TPU v7x, 128 devices: a whole 4x4x4 slice. The times are simulated.
128 devices in a mesh: tile: 64 (over x, y, z_lo, core), sub: 2 (over z_hi).
Axes of the slice: x: 4, y: 4, z: 4 (z_hi: 2, z_lo: 2; z = z_hi * 2 + z_lo), core: 2. Of those that a mesh axis runs over, the one named last changes fastest.
Arguments:
- adjoint_flux: bfloat16 [6, 7, 2097152], P(None, None, ('tile', 'sub')), may hold values from -6 to 6
- ocean_wet: int32 [2097152], P(('tile', 'sub')), may hold values 0 or 1
- intersection_weight: bfloat16 [16384, 2, 128, 128], P(('tile', 'sub')), may hold values from -0.5 to 0.5
- pair_owner: int32 [16384, 2], P(('tile', 'sub')), may hold values from 0 to 127, all different within a row; in each aligned block of 128 rows (0 to 127, 128 to 255, ...) at most 4 rows name the same one
- pair_block: int32 [16384, 2], P(('tile', 'sub')), may hold values from 0 to 179
- land_sea: int32 [2048, 1440], P('tile', 'sub'), may hold values 0 or 1
- east_coef: float32 [2048, 1440], P('tile', 'sub'), may hold values from 0.03 to 0.24
- north_coef: float32 [2048, 1440], P('tile', 'sub'), may hold values from 0.03 to 0.24
Outputs:
- smoothed: float32 [14, 2048, 1440], P(None, 'tile', 'sub')
Inputs may be any that keep to these rules, and one draw needn't show every extreme that they name: `pair_owner`: for each ocean block its 2 entries name different owners; among the rows of one device's 128 ocean blocks no owner is named more than 4 times, a bound that some block reaches. `pair_block`: control blocks of an owner are 8 rows by 16 longitudes, numbered along longitude first.
All inputs are finite; a program needn't handle non-finite values. No bound on the sum of `ocean_wet` or of `land_sea` on one device may be relied on, other than what follows from the above.
Results may differ from a plain program's by a relative error of at most 0.0029.
Values sent between devices are 32-bit elements; how exact they have to be, the bound alone decides.
A program may use at most 128 MiB of HBM per device.

v0:
```python
import jax
import jax.numpy as jnp
from jax import lax
from jax.sharding import PartitionSpec as P

PASSES = 4


def with_halo(value, sides, width, wrap):
    for axis, dim in sides:
        peers, length = (lax.axis_size(axis), value.shape[dim])
        up = [(i, (i + 1) % peers) for i in range(peers if wrap else peers - 1)]
        down = [(j, i) for i, j in up]
        last = lax.slice_in_dim(value, length - width, length, axis=dim)
        initial = lax.slice_in_dim(value, 0, width, axis=dim)
        before = lax.ppermute(last, axis, up)
        after = lax.ppermute(initial, axis, down)
        value = jnp.concatenate([before, value, after], axis=dim)
    return value


def hour_weights(hours):
    frac = jnp.arange(hours, dtype=jnp.float32) / hours
    return jnp.stack([1.0 - frac, frac])


def smooth_once(field, east, north):
    inner = field[:, 1:-1, 1:-1]
    east_flux = east[1:-1, :-1] * (field[:, 1:-1, 1:] - field[:, 1:-1, :-1])
    north_flux = north[:-1, 1:-1] * (field[:, 1:, 1:-1] - field[:, :-1, 1:-1])
    return (
        inner
        + (east_flux[:, :, 1:] - east_flux[:, :, :-1])
        + (north_flux[:, 1:, :] - north_flux[:, :-1, :])
    )


def scatter_blocks(pieces, blocks_dev):
    values, labels = pieces
    values = values.reshape((-1,) + values.shape[-2:])
    labels = labels.reshape((-1, labels.shape[-1]))
    picked = (labels[:, :, None] == jnp.arange(blocks_dev, dtype=jnp.float32)).astype(jnp.float32)
    return jnp.einsum("skb,skc->bkc", picked, values, precision=lax.Precision.HIGHEST)


def on_device(
    adjoint_flux,
    ocean_wet,
    intersection_weight,
    pair_owner,
    pair_block,
    land_sea,
    east_coef,
    north_coef,
):
    hours, fields, cells = adjoint_flux.shape
    blocks_here, intersections, width, _ = intersection_weight.shape
    channels = 2 * fields
    tiles = lax.axis_size("tile")
    halves = lax.axis_size("sub")
    devices = tiles * halves
    capacity = (blocks_here * intersections + devices - 1) // devices * 2
    rows, cols = land_sea.shape
    band = width // 8
    across = cols // band
    blocks_dev = rows // 8 * across
    weights = hour_weights(hours)
    summed = jnp.zeros((2, fields, cells), jnp.float32)
    for hour in range(hours):
        summed = (
            summed + weights[:, hour][:, None, None] * adjoint_flux[hour].astype(jnp.float32)[None]
        )
    timed = (
        (summed * ocean_wet.astype(jnp.float32))
        .reshape(channels, blocks_here, width)
        .astype(jnp.bfloat16)
    )
    contributions = jnp.einsum(
        "hpo,pkoc->pkhc", timed, intersection_weight, preferred_element_type=jnp.float32
    )
    contributions = contributions.reshape(blocks_here * intersections, channels, width)
    owners = pair_owner.reshape(-1)
    targets = pair_block.reshape(-1)
    chosen = (owners[:, None] == jnp.arange(devices, dtype=jnp.int32)[None, :]).astype(jnp.int32)
    before = jnp.cumsum(chosen, axis=0) - chosen
    ranking = jnp.sum(before * chosen, axis=1)
    slots = owners * capacity + ranking
    outgoing = (
        jnp.zeros((devices * capacity, channels, width), jnp.float32).at[slots].set(contributions)
    )
    labels = (
        jnp.full((devices * capacity,), -1.0, jnp.float32)
        .at[slots]
        .set(targets.astype(jnp.float32))
    )
    labels = jnp.broadcast_to(labels[:, None], (devices * capacity, channels))
    shaped = (
        outgoing.reshape(devices, capacity, channels, width),
        labels.reshape(devices, capacity, channels),
    )
    blocks = scatter_blocks(
        (
            lax.all_to_all(shaped[0], ("tile", "sub"), split_axis=0, concat_axis=0, tiled=True),
            lax.all_to_all(shaped[1], ("tile", "sub"), split_axis=0, concat_axis=0, tiled=True),
        ),
        blocks_dev,
    )
    grid = (
        blocks.reshape(rows // 8, across, channels, 8, band)
        .transpose(2, 0, 3, 1, 4)
        .reshape(channels, rows, cols)
    )
    masked = grid * land_sea.astype(jnp.float32)
    row_global = lax.axis_index("tile") * rows + jnp.arange(rows, dtype=jnp.int32)
    north_open = jnp.where(row_global[:, None] < tiles * rows - 1, north_coef, jnp.float32(0.0))
    stacked = jnp.concatenate([masked, east_coef[None], north_open[None]], axis=0)
    extended = with_halo(stacked, (("tile", 1),), 1, False)
    extended = with_halo(extended, (("sub", 2),), 1, True)
    east = extended[channels]
    north = extended[channels + 1]
    field = smooth_once(extended[:channels], east, north)
    for turn in range(1, PASSES):
        padded = with_halo(field, (("tile", 1),), 1, False)
        padded = with_halo(padded, (("sub", 2),), 1, True)
        field = smooth_once(padded, east, north)
    return field


def solution(mesh):
    in_specs = (
        P(None, None, ("tile", "sub")),
        P(("tile", "sub")),
        P(("tile", "sub"), None, None, None),
        P(("tile", "sub"), None),
        P(("tile", "sub"), None),
        P("tile", "sub"),
        P("tile", "sub"),
        P("tile", "sub"),
    )
    out_specs = P(None, "tile", "sub")
    return jax.shard_map(
        on_device, mesh=mesh, in_specs=in_specs, out_specs=out_specs, check_vma=False
    )
```

profile of v0, /device:TPU:4, one launch (start us, length us, event | category | flops | bytes accessed | tf_op | source)
XLA Modules:
  0.0 260.2 jit_solution(1551108744213798158)
XLA Ops:
  3.6 1.4 scatter_custom_fusion.1
  6.0 11.0 %all-to-all-start.1 = ((f32[128,4,14]{2,1,0:T(4,128)}), f32[128,4,14]{2,1,0:T(4,128)}, u32[]{:S(2)}, u32[]{:S(2)}) async-start(f32[128,4,14]{2,1,0:T(4,128)} %broadcast_in_dim.27), calls=%async_computation.1 | async-start | bytes 524288 | tf_op jit(solution)/shard_map/all_to_all | solution.py:104
  18.2 2.6 bitcast_convert_fusion.5
  21.9 1.1 mul.283
  23.0 1.4 mul.284
  24.4 1.1 mul.292
  25.5 1.4 mul.293
  26.9 1.1 mul.301
  28.1 1.4 mul.302
  29.5 1.4 mul.311
  31.0 2.6 %fusion.26 = bf16[14,128,128,1]{2,1,0,3:T(8,128)(2,1)S(1)} fusion(f32[128,128]{1,0:T(8,128)S(1)} %convert_bitcast_fusion, f32[14,128,128]{2,1,0:T(8,128)} %mul.311, f32[14]{0:T(128)S(1)} %mul.306, f32[14,128,128]{2,1,0:T(8,128)} %mul.302, f32[14]{0:T(128)S(1)} %mul.297, f32[14,128,128]{2,1,0:T(8,128)} %mul.293, f32[14]{0:T(128)S(1)} %mul.288, ...), kind=kLoop, calls=%fused_computation.76 | loop fusion | flops 2981888 | bytes 6029648 | tf_op jit(solution)/shard_map/convert_element_type | solution.py:76
  33.6 4.7 %fusion.24 = f32[128,14,2,128]{3,1,2,0:T(8,128)S(1)} fusion(bf16[128,2,128,128]{3,2,1,0:T(8,128)(2,1)} %param.10, bf16[14,128,128,1]{2,1,0,3:T(8,128)(2,1)S(1)} %fusion.26), kind=kOutput, calls=%fused_computation.74 | convolution fusion | flops 117440512 | bytes 10682368 | tf_op jit(solution)/shard_map/hpo,pkoc->pkhc/dot_general | solution.py:78
  38.3 2.2 broadcast_in_dim.20
  40.5 26.5 %scatter_fusion = f32[512,14,128]{2,1,0:T(8,128)} fusion(f32[512,14,128]{2,1,0:T(8,128)} %broadcast_in_dim.20, s32[256]{0:T(256)S(1)} %bitcast.71, f32[256,14,128]{2,1,0:T(8,128)S(1)} %bitcast.58), kind=kCustom, calls=%fused_computation | custom fusion | bytes 5506048 | tf_op jit(solution)/shard_map/scatter | solution.py:89
  67.0 5.8 %copy.39 = f32[128,4,14,128]{3,1,2,0:T(4,128)} copy(f32[128,4,14,128]{3,2,1,0:T(8,128)} %bitcast.57) | data formatting | bytes 7340032 | tf_op jit(solution)/shard_map/reshape | solution.py:98
  72.8 10.2 %all-to-all-start = ((f32[128,4,14,128]{3,1,2,0:T(4,128)}), f32[128,4,14,128]{3,1,2,0:T(4,128)}, u32[]{:S(2)}, u32[]{:S(2)}) async-start(f32[128,4,14,128]{3,1,2,0:T(4,128)} %copy.39), calls=%async_computation | async-start | bytes 7340032 | tf_op jit(solution)/shard_map/all_to_all | solution.py:103
  84.2 44.5 %all-to-all-done = f32[128,4,14,128]{3,1,2,0:T(4,128)} async-done(((f32[128,4,14,128]{3,1,2,0:T(4,128)}), f32[128,4,14,128]{3,1,2,0:T(4,128)}, u32[]{:S(2)}, u32[]{:S(2)}) %all-to-all-start) | async-done | bytes 3670048 | tf_op jit(solution)/shard_map/all_to_all | solution.py:103
  128.7 3.0 %copy.40 = f32[128,4,14,128]{3,1,0,2:T(4,128)S(1)} copy(f32[128,4,14,128]{3,1,2,0:T(4,128)} %all-to-all-done) | data formatting | bytes 7340032 | tf_op jit(solution)/shard_map/all_to_all | solution.py:103
  131.6 2.9 %fusion.7 = f32[180,14,128]{2,0,1:T(8,128)S(1)} fusion(f32[512,14,128]{2,0,1:T(8,128)S(1)} %bitcast.59, f32[512,14]{0,1:T(8,128)S(1)} %copy.42), kind=kOutput, calls=%fused_computation.19 | convolution fusion | flops 1983098880 | bytes 4988928 | tf_op jit(solution)/shard_map/skb,skc->bkc/dot_general | solution.py:43
  135.2 3.0 %reshape.117 = f32[4,45,14,8,16]{1,0,4,3,2:T(4,128)} reshape(f32[180,14,128]{0,2,1:T(8,128)S(1)} %copy.43) | data formatting | bytes 2580480 | tf_op jit(solution)/shard_map/reshape | solution.py:109
  138.3 9.0 %copy.44 = f32[14,4,8,45,16]{4,3,2,1,0:T(8,128)} copy(f32[14,4,8,45,16]{3,1,4,2,0:T(4,128)} %bitcast.60) | data formatting | bytes 2580480 | tf_op jit(solution)/shard_map/transpose | solution.py:110
  147.3 7.3 %reshape.118 = f32[14,32,720]{2,1,0:T(8,128)S(1)} reshape(f32[14,4,8,45,16]{4,3,2,1,0:T(8,128)} %copy.44) | data formatting | bytes 2580480 | tf_op jit(solution)/shard_map/reshape | solution.py:111
  155.6 1.9 collective-permute-start
  157.5 6.7 %collective-permute-start.1 = (f32[16,1,720]{2,1,0:T(1,128)S(1)}, f32[16,1,720]{2,1,0:T(1,128)S(1)}, u32[]{:S(2)}, u32[]{:S(2)}) collective-permute-start(f32[16,1,720]{2,1,0:T(1,128)S(1)} %get-tuple-element.15), channel_id=1, source_target_pairs={{2,0},{4,2},{6,4},{8,6},{10,8},{12,10},{14,12},{16,14},{18,16},{20... | collective-permute-start | bytes 138248 | tf_op jit(solution)/shard_map/ppermute | solution.py:17
  164.2 1.7 collective-permute-done.1
  166.1 1.7 collective-permute-start.2
  167.7 1.9 collective-permute-start.3
  169.7 7.9 %collective-permute-done.2 = f32[16,34,1]{2,1,0:T(8,128)S(1)} collective-permute-done((f32[16,34,1]{2,1,0:T(8,128)S(1)}, f32[16,34,1]{2,1,0:T(8,128)S(1)}, u32[]{:S(2)}, u32[]{:S(2)}) %collective-permute-start.2) | collective-permute-done | bytes 2208 | tf_op jit(solution)/shard_map/ppermute | solution.py:16
  177.6 3.5 %collective-permute-done.3 = f32[16,34,1]{2,1,0:T(8,128)S(1)} collective-permute-done((f32[16,34,1]{2,1,0:T(8,128)S(1)}, f32[16,34,1]{2,1,0:T(8,128)S(1)}, u32[]{:S(2)}, u32[]{:S(2)}) %collective-permute-start.3) | collective-permute-done | bytes 2208 | tf_op jit(solution)/shard_map/ppermute | solution.py:17
  182.8 1.9 collective-permute-start.4
  184.7 6.7 %collective-permute-start.5 = (f32[14,1,720]{2,1,0:T(1,128)S(1)}, f32[14,1,720]{2,1,0:T(1,128)S(1)}, u32[]{:S(2)}, u32[]{:S(2)}) collective-permute-start(f32[14,1,720]{2,1,0:T(1,128)S(1)} %get-tuple-element.34), channel_id=1, source_target_pairs={{2,0},{4,2},{6,4},{8,6},{10,8},{12,10},{14,12},{16,14},{18,16},{20... | collective-permute-start | bytes 120968 | tf_op jit(solution)/shard_map/ppermute | solution.py:17
  191.4 1.7 collective-permute-done.5
  193.2 3.3 %collective-permute-start.6 = (f32[14,34,1]{2,1,0:T(8,128)S(1)}, f32[14,34,1]{2,1,0:T(8,128)S(1)}, u32[]{:S(2)}, u32[]{:S(2)}) collective-permute-start(f32[14,34,1]{2,1,0:T(8,128)S(1)} %get-tuple-element.27), channel_id=1, source_target_pairs={{1,0},{0,1},{3,2},{2,3},{5,4},{4,5},{7,6},{6,7},{9,8},{8,9},{11,10... | collective-permute-start | bytes 5720 | tf_op jit(solution)/shard_map/ppermute | solution.py:17
  197.1 7.5 %collective-permute-done.6 = f32[14,34,1]{2,1,0:T(8,128)S(1)} collective-permute-done((f32[14,34,1]{2,1,0:T(8,128)S(1)}, f32[14,34,1]{2,1,0:T(8,128)S(1)}, u32[]{:S(2)}, u32[]{:S(2)}) %collective-permute-start.6) | collective-permute-done | bytes 1936 | tf_op jit(solution)/shard_map/ppermute | solution.py:17
  204.6 3.3 %collective-permute-done.7 = f32[14,34,1]{2,1,0:T(8,128)S(1)} collective-permute-done((f32[14,34,1]{2,1,0:T(8,128)S(1)}, f32[14,34,1]{2,1,0:T(8,128)S(1)}, u32[]{:S(2)}, u32[]{:S(2)}) %collective-permute-start.7) | collective-permute-done | bytes 1936 | tf_op jit(solution)/shard_map/ppermute | solution.py:16
  209.1 1.9 collective-permute-start.8
  211.0 6.7 %collective-permute-start.9 = (f32[14,1,720]{2,1,0:T(1,128)S(1)}, f32[14,1,720]{2,1,0:T(1,128)S(1)}, u32[]{:S(2)}, u32[]{:S(2)}) collective-permute-start(f32[14,1,720]{2,1,0:T(1,128)S(1)} %get-tuple-element.32), channel_id=1, source_target_pairs={{2,0},{4,2},{6,4},{8,6},{10,8},{12,10},{14,12},{16,14},{18,16},{20... | collective-permute-start | bytes 120968 | tf_op jit(solution)/shard_map/ppermute | solution.py:17
  217.7 1.7 collective-permute-done.9
  219.5 3.3 %collective-permute-start.10 = (f32[14,34,1]{2,1,0:T(8,128)S(1)}, f32[14,34,1]{2,1,0:T(8,128)S(1)}, u32[]{:S(2)}, u32[]{:S(2)}) collective-permute-start(f32[14,34,1]{2,1,0:T(8,128)S(1)} %get-tuple-element.25), channel_id=1, source_target_pairs={{1,0},{0,1},{3,2},{2,3},{5,4},{4,5},{7,6},{6,7},{9,8},{8,9},{11,10... | collective-permute-start | bytes 5720 | tf_op jit(solution)/shard_map/ppermute | solution.py:17
  223.4 6.6 %collective-permute-done.10 = f32[14,34,1]{2,1,0:T(8,128)S(1)} collective-permute-done((f32[14,34,1]{2,1,0:T(8,128)S(1)}, f32[14,34,1]{2,1,0:T(8,128)S(1)}, u32[]{:S(2)}, u32[]{:S(2)}) %collective-permute-start.10) | collective-permute-done | bytes 1936 | tf_op jit(solution)/shard_map/ppermute | solution.py:17
  230.0 3.1 %collective-permute-done.11 = f32[14,34,1]{2,1,0:T(8,128)S(1)} collective-permute-done((f32[14,34,1]{2,1,0:T(8,128)S(1)}, f32[14,34,1]{2,1,0:T(8,128)S(1)}, u32[]{:S(2)}, u32[]{:S(2)}) %collective-permute-start.11) | collective-permute-done | bytes 1936 | tf_op jit(solution)/shard_map/ppermute | solution.py:16
  234.3 1.9 collective-permute-start.12
  236.2 6.7 %collective-permute-start.13 = (f32[14,1,720]{2,1,0:T(1,128)S(1)}, f32[14,1,720]{2,1,0:T(1,128)S(1)}, u32[]{:S(2)}, u32[]{:S(2)}) collective-permute-start(f32[14,1,720]{2,1,0:T(1,128)S(1)} %get-tuple-element.30), channel_id=1, source_target_pairs={{2,0},{4,2},{6,4},{8,6},{10,8},{12,10},{14,12},{16,14},{18,16},{20... | collective-permute-start | bytes 120968 | tf_op jit(solution)/shard_map/ppermute | solution.py:17
  242.9 1.7 collective-permute-done.13
  244.7 3.3 %collective-permute-start.14 = (f32[14,34,1]{2,1,0:T(8,128)S(1)}, f32[14,34,1]{2,1,0:T(8,128)S(1)}, u32[]{:S(2)}, u32[]{:S(2)}) collective-permute-start(f32[14,34,1]{2,1,0:T(8,128)S(1)} %get-tuple-element.23), channel_id=1, source_target_pairs={{1,0},{0,1},{3,2},{2,3},{5,4},{4,5},{7,6},{6,7},{9,8},{8,9},{11,10... | collective-permute-start | bytes 5720 | tf_op jit(solution)/shard_map/ppermute | solution.py:17
  248.6 6.4 %collective-permute-done.14 = f32[14,34,1]{2,1,0:T(8,128)S(1)} collective-permute-done((f32[14,34,1]{2,1,0:T(8,128)S(1)}, f32[14,34,1]{2,1,0:T(8,128)S(1)}, u32[]{:S(2)}, u32[]{:S(2)}) %collective-permute-start.14) | collective-permute-done | bytes 1936 | tf_op jit(solution)/shard_map/ppermute | solution.py:17
  255.0 3.1 %collective-permute-done.15 = f32[14,34,1]{2,1,0:T(8,128)S(1)} collective-permute-done((f32[14,34,1]{2,1,0:T(8,128)S(1)}, f32[14,34,1]{2,1,0:T(8,128)S(1)}, u32[]{:S(2)}, u32[]{:S(2)}) %collective-permute-start.15) | collective-permute-done | bytes 1936 | tf_op jit(solution)/shard_map/ppermute | solution.py:16
  258.7 1.5 fusion.8
  (86 shorter events, 16.7 us)
Async XLA Ops:
  6.0 66.7 %all-to-all-start.1 = ((f32[128,4,14]{2,1,0:T(4,128)}), f32[128,4,14]{2,1,0:T(4,128)}, u32[]{:S(2)}, u32[]{:S(2)}) async-start(f32[128,4,14]{2,1,0:T(4,128)} %broadcast_in_dim.27), calls=%async_computation.1 | async-start | bytes 524288 | tf_op jit(solution)/shard_map/all_to_all | solution.py:104
  29.5 1.5 copy-start.3
  72.8 10.2 %copy-start.1 = (s32[32,720]{1,0:T(8,128)S(1)}, s32[32,720]{1,0:T(8,128)}, u32[]{:S(2)}) copy-start(s32[32,720]{1,0:T(8,128)} %param.13) | copy-start | bytes 276484
  72.8 10.2 %copy-start.2 = (f32[32,720]{1,0:T(8,128)S(1)}, f32[32,720]{1,0:T(8,128)}, u32[]{:S(2)}) copy-start(f32[32,720]{1,0:T(8,128)} %param.15) | copy-start | bytes 276484
  72.8 55.9 %all-to-all-start = ((f32[128,4,14,128]{3,1,2,0:T(4,128)}), f32[128,4,14,128]{3,1,2,0:T(4,128)}, u32[]{:S(2)}, u32[]{:S(2)}) async-start(f32[128,4,14,128]{3,1,2,0:T(4,128)} %copy.39), calls=%async_computation | async-start | bytes 7340032 | tf_op jit(solution)/shard_map/all_to_all | solution.py:103
  154.6 0.9 copy-start
  155.6 8.6 %collective-permute-start = (f32[16,1,720]{2,1,0:T(1,128)S(1)}, f32[16,1,720]{2,1,0:T(1,128)S(1)}, u32[]{:S(2)}, u32[]{:S(2)}) collective-permute-start(f32[16,1,720]{2,1,0:T(1,128)S(1)} %get-tuple-element.16), channel_id=1, source_target_pairs={{0,2},{2,4},{4,6},{6,8},{8,10},{10,12},{12,14},{14,16},{16,18},{18... | collective-permute-start | bytes 138248 | tf_op jit(solution)/shard_map/ppermute | solution.py:16
  157.5 8.4 %collective-permute-start.1 = (f32[16,1,720]{2,1,0:T(1,128)S(1)}, f32[16,1,720]{2,1,0:T(1,128)S(1)}, u32[]{:S(2)}, u32[]{:S(2)}) collective-permute-start(f32[16,1,720]{2,1,0:T(1,128)S(1)} %get-tuple-element.15), channel_id=1, source_target_pairs={{2,0},{4,2},{6,4},{8,6},{10,8},{12,10},{14,12},{16,14},{18,16},{20... | collective-permute-start | bytes 138248 | tf_op jit(solution)/shard_map/ppermute | solution.py:17
  166.1 11.5 %collective-permute-start.2 = (f32[16,34,1]{2,1,0:T(8,128)S(1)}, f32[16,34,1]{2,1,0:T(8,128)S(1)}, u32[]{:S(2)}, u32[]{:S(2)}) collective-permute-start(f32[16,34,1]{2,1,0:T(8,128)S(1)} %get-tuple-element.13), channel_id=1, source_target_pairs={{0,1},{1,0},{2,3},{3,2},{4,5},{5,4},{6,7},{7,6},{8,9},{9,8},{10,11... | collective-permute-start | bytes 6536 | tf_op jit(solution)/shard_map/ppermute | solution.py:16
  167.7 13.3 %collective-permute-start.3 = (f32[16,34,1]{2,1,0:T(8,128)S(1)}, f32[16,34,1]{2,1,0:T(8,128)S(1)}, u32[]{:S(2)}, u32[]{:S(2)}) collective-permute-start(f32[16,34,1]{2,1,0:T(8,128)S(1)} %get-tuple-element.14), channel_id=1, source_target_pairs={{1,0},{0,1},{3,2},{2,3},{5,4},{4,5},{7,6},{6,7},{9,8},{8,9},{11,10... | collective-permute-start | bytes 6536 | tf_op jit(solution)/shard_map/ppermute | solution.py:17
  182.8 8.6 %collective-permute-start.4 = (f32[14,1,720]{2,1,0:T(1,128)S(1)}, f32[14,1,720]{2,1,0:T(1,128)S(1)}, u32[]{:S(2)}, u32[]{:S(2)}) collective-permute-start(f32[14,1,720]{2,1,0:T(1,128)S(1)} %get-tuple-element.33), channel_id=1, source_target_pairs={{0,2},{2,4},{4,6},{6,8},{8,10},{10,12},{12,14},{14,16},{16,18},{18... | collective-permute-start | bytes 120968 | tf_op jit(solution)/shard_map/ppermute | solution.py:16
  184.7 8.3 %collective-permute-start.5 = (f32[14,1,720]{2,1,0:T(1,128)S(1)}, f32[14,1,720]{2,1,0:T(1,128)S(1)}, u32[]{:S(2)}, u32[]{:S(2)}) collective-permute-start(f32[14,1,720]{2,1,0:T(1,128)S(1)} %get-tuple-element.34), channel_id=1, source_target_pairs={{2,0},{4,2},{6,4},{8,6},{10,8},{12,10},{14,12},{16,14},{18,16},{20... | collective-permute-start | bytes 120968 | tf_op jit(solution)/shard_map/ppermute | solution.py:17
  193.2 11.4 %collective-permute-start.6 = (f32[14,34,1]{2,1,0:T(8,128)S(1)}, f32[14,34,1]{2,1,0:T(8,128)S(1)}, u32[]{:S(2)}, u32[]{:S(2)}) collective-permute-start(f32[14,34,1]{2,1,0:T(8,128)S(1)} %get-tuple-element.27), channel_id=1, source_target_pairs={{1,0},{0,1},{3,2},{2,3},{5,4},{4,5},{7,6},{6,7},{9,8},{8,9},{11,10... | collective-permute-start | bytes 5720 | tf_op jit(solution)/shard_map/ppermute | solution.py:17
  196.6 11.3 %collective-permute-start.7 = (f32[14,34,1]{2,1,0:T(8,128)S(1)}, f32[14,34,1]{2,1,0:T(8,128)S(1)}, u32[]{:S(2)}, u32[]{:S(2)}) collective-permute-start(f32[14,34,1]{2,1,0:T(8,128)S(1)} %get-tuple-element.28), channel_id=1, source_target_pairs={{0,1},{1,0},{2,3},{3,2},{4,5},{5,4},{6,7},{7,6},{8,9},{9,8},{10,11... | collective-permute-start | bytes 5720 | tf_op jit(solution)/shard_map/ppermute | solution.py:16
  209.1 8.6 %collective-permute-start.8 = (f32[14,1,720]{2,1,0:T(1,128)S(1)}, f32[14,1,720]{2,1,0:T(1,128)S(1)}, u32[]{:S(2)}, u32[]{:S(2)}) collective-permute-start(f32[14,1,720]{2,1,0:T(1,128)S(1)} %get-tuple-element.31), channel_id=1, source_target_pairs={{0,2},{2,4},{4,6},{6,8},{8,10},{10,12},{12,14},{14,16},{16,18},{18... | collective-permute-start | bytes 120968 | tf_op jit(solution)/shard_map/ppermute | solution.py:16
  211.0 8.3 %collective-permute-start.9 = (f32[14,1,720]{2,1,0:T(1,128)S(1)}, f32[14,1,720]{2,1,0:T(1,128)S(1)}, u32[]{:S(2)}, u32[]{:S(2)}) collective-permute-start(f32[14,1,720]{2,1,0:T(1,128)S(1)} %get-tuple-element.32), channel_id=1, source_target_pairs={{2,0},{4,2},{6,4},{8,6},{10,8},{12,10},{14,12},{16,14},{18,16},{20... | collective-permute-start | bytes 120968 | tf_op jit(solution)/shard_map/ppermute | solution.py:17
  219.5 10.6 %collective-permute-start.10 = (f32[14,34,1]{2,1,0:T(8,128)S(1)}, f32[14,34,1]{2,1,0:T(8,128)S(1)}, u32[]{:S(2)}, u32[]{:S(2)}) collective-permute-start(f32[14,34,1]{2,1,0:T(8,128)S(1)} %get-tuple-element.25), channel_id=1, source_target_pairs={{1,0},{0,1},{3,2},{2,3},{5,4},{4,5},{7,6},{6,7},{9,8},{8,9},{11,10... | collective-permute-start | bytes 5720 | tf_op jit(solution)/shard_map/ppermute | solution.py:17
  222.8 10.3 %collective-permute-start.11 = (f32[14,34,1]{2,1,0:T(8,128)S(1)}, f32[14,34,1]{2,1,0:T(8,128)S(1)}, u32[]{:S(2)}, u32[]{:S(2)}) collective-permute-start(f32[14,34,1]{2,1,0:T(8,128)S(1)} %get-tuple-element.26), channel_id=1, source_target_pairs={{0,1},{1,0},{2,3},{3,2},{4,5},{5,4},{6,7},{7,6},{8,9},{9,8},{10,11... | collective-permute-start | bytes 5720 | tf_op jit(solution)/shard_map/ppermute | solution.py:16
  234.3 8.6 %collective-permute-start.12 = (f32[14,1,720]{2,1,0:T(1,128)S(1)}, f32[14,1,720]{2,1,0:T(1,128)S(1)}, u32[]{:S(2)}, u32[]{:S(2)}) collective-permute-start(f32[14,1,720]{2,1,0:T(1,128)S(1)} %get-tuple-element.29), channel_id=1, source_target_pairs={{0,2},{2,4},{4,6},{6,8},{8,10},{10,12},{12,14},{14,16},{16,18},{18... | collective-permute-start | bytes 120968 | tf_op jit(solution)/shard_map/ppermute | solution.py:16
  236.2 8.3 %collective-permute-start.13 = (f32[14,1,720]{2,1,0:T(1,128)S(1)}, f32[14,1,720]{2,1,0:T(1,128)S(1)}, u32[]{:S(2)}, u32[]{:S(2)}) collective-permute-start(f32[14,1,720]{2,1,0:T(1,128)S(1)} %get-tuple-element.30), channel_id=1, source_target_pairs={{2,0},{4,2},{6,4},{8,6},{10,8},{12,10},{14,12},{16,14},{18,16},{20... | collective-permute-start | bytes 120968 | tf_op jit(solution)/shard_map/ppermute | solution.py:17
  244.7 10.3 %collective-permute-start.14 = (f32[14,34,1]{2,1,0:T(8,128)S(1)}, f32[14,34,1]{2,1,0:T(8,128)S(1)}, u32[]{:S(2)}, u32[]{:S(2)}) collective-permute-start(f32[14,34,1]{2,1,0:T(8,128)S(1)} %get-tuple-element.23), channel_id=1, source_target_pairs={{1,0},{0,1},{3,2},{2,3},{5,4},{4,5},{7,6},{6,7},{9,8},{8,9},{11,10... | collective-permute-start | bytes 5720 | tf_op jit(solution)/shard_map/ppermute | solution.py:17
  248.0 10.1 %collective-permute-start.15 = (f32[14,34,1]{2,1,0:T(8,128)S(1)}, f32[14,34,1]{2,1,0:T(8,128)S(1)}, u32[]{:S(2)}, u32[]{:S(2)}) collective-permute-start(f32[14,34,1]{2,1,0:T(8,128)S(1)} %get-tuple-element.24), channel_id=1, source_target_pairs={{0,1},{1,0},{2,3},{3,2},{4,5},{5,4},{6,7},{7,6},{8,9},{9,8},{10,11... | collective-permute-start | bytes 5720 | tf_op jit(solution)/shard_map/ppermute | solution.py:16
where the time goes:
time: 262 us; the launch traced here: 260 us
  waiting for transfers between devices  92.6 us (35%)
  local copies, waits for them, and re-layouts  75.1 us (29%)
  starting transfers between devices  69.9 us (27%)
  other arithmetic  14.6 us (6%)
  matrix products  7.59 us (3%)
    all_to_all x1, waiting for transfers between devices, on_device(): lax.all_to_all(shaped[0], ('tile', 'sub'), split_axis=0, concat_axis=0, t...  44.5 us
    ppermute x8, starting transfers between devices, with_halo(): after = lax.ppermute(initial, axis, down)  38.5 us
    ppermute x8, waiting for transfers between devices, with_halo(): after = lax.ppermute(initial, axis, down)  30.7 us
    scatter x1, local copies, waits for them, and re-layouts, on_device(): jnp.zeros((devices * capacity, channels, width), jnp.float32).at[slots]  26.5 us
    ppermute x8, waiting for transfers between devices, with_halo(): before = lax.ppermute(last, axis, up)  17.4 us
    mul x24, local copies, waits for them, and re-layouts, on_device(): weights[:, hour][:, None, None]  11 us
    all_to_all x1, starting transfers between devices, on_device(): lax.all_to_all(shaped[1], ('tile', 'sub'), split_axis=0, concat_axis=0, t...  11 us
    ppermute x8, starting transfers between devices, with_halo(): before = lax.ppermute(last, axis, up)  10.2 us
  transfers between devices with their start and end apart: 18, of which 13 were waited for; matrix products, arithmetic and copies ran while one was open for 22% of the time, Pallas kernels for 0%

commit v1 on v0

v1 whole, which is shorter than its diff:
```python
import functools

import jax
import jax.numpy as jnp
import numpy as np
from jax import lax
from jax.experimental import pallas as pl
from jax.experimental.pallas import tpu as pltpu
from jax.sharding import PartitionSpec as P

PASSES = 4
HALO = 4
CAP = 4
HOURS = 6
FIELDS = 7
BLK = 128
OB = 128
ROWS = 32
COLS = 720
ACROSS = 45
WIDE = 48
VR = ROWS + 8
VC = 768
DEV = 128
STRIDE = 37
W_CHUNKS = 8
F_CHUNKS = 4
MESH = pl.DeviceIdType.MESH
F32 = jnp.float32
BF16 = jnp.bfloat16


def iota(shape, dim):
    return lax.broadcasted_iota(jnp.int32, shape, dim)


def peer_of(tile, sub, j):
    o = (j * STRIDE) % DEV
    x = (tile // 16 + o // 32) % 4
    y = ((tile // 4) % 4 + (o // 8) % 4) % 4
    z = (sub * 2 + (tile // 2) % 2 + (o // 2) % 4) % 4
    c = (tile % 2 + o % 2) % 2
    return ((x * 4 + y) * 2 + z % 2) * 2 + c, z // 2


def swap_lanes_rows(x):
    s = iota(x.shape, 1)
    g = iota(x.shape, 2) // 16
    for m in (4, 2, 1):
        sb = (s // m) % 2
        gb = (g // m) % 2
        up = pltpu.roll(pltpu.roll(x, 16 * m, 2), 8 - m, 1)
        down = up if m == 4 else pltpu.roll(pltpu.roll(x, 128 - 16 * m, 2), m, 1)
        x = jnp.where(sb < gb, up, jnp.where(sb > gb, down, x))
    return x


def halo_start(v, count, tile, sub, row_out, row_in, col_out, col_in, cor_in, send, recv):
    low = iota((8, VC), 0) < HALO
    for i in range((count + 1) // 2):
        a, b = 2 * i, min(2 * i + 1, count - 1)
        row_out[0, i] = jnp.where(low, pltpu.roll(v[a, 24:32, :], 4, 0), v[b, 24:32, :])
        row_out[1, i] = jnp.where(low, v[a, 0:8, :], pltpu.roll(v[b, 0:8, :], 4, 0))
    lane = iota((ROWS, 128), 1)
    edge = jnp.zeros((ROWS, 128), F32)
    for f in range(count):
        left = v[f, 0:ROWS, 0:128]
        right = v[f, 0:ROWS, 640:768]
        if f:
            left = pltpu.roll(left, 8 * f, 1)
        right = pltpu.roll(right, (8 * f + 4 - 76) % 128, 1)
        edge = jnp.where((lane >= 8 * f) & (lane < 8 * f + 4), left, edge)
        edge = jnp.where((lane >= 8 * f + 4) & (lane < 8 * f + 8), right, edge)
    col_out[...] = edge
    up, down, other = (tile + 1) % 64, (tile + 63) % 64, 1 - sub
    n = (count + 1) // 2
    parts = (
        (row_out.at[0, pl.ds(0, n)], row_in.at[0, pl.ds(0, n)], (up, sub)),
        (row_out.at[1, pl.ds(0, n)], row_in.at[1, pl.ds(0, n)], (down, sub)),
        (col_out, col_in, (tile, other)),
        (col_out.at[pl.ds(24, 8)], cor_in.at[0], (up, other)),
        (col_out.at[pl.ds(0, 8)], cor_in.at[1], (down, other)),
    )
    copies = []
    for i, (src, dst, to) in enumerate(parts):
        copy = pltpu.make_async_remote_copy(
            src_ref=src,
            dst_ref=dst,
            send_sem=send.at[i],
            recv_sem=recv.at[i],
            device_id=to,
            device_id_type=MESH,
        )
        copy.start()
        copies.append(copy)
    return copies


def halo_finish(copies, v, count, row_in, col_in, cor_in):
    for copy in copies:
        copy.wait()
    low = iota((8, VC), 0) < HALO
    for i in range((count + 1) // 2):
        south, north = row_in[1, i], row_in[0, i]
        v[2 * i, ROWS:VR, :] = jnp.where(low, south, pltpu.roll(north, 4, 0))
        if 2 * i + 1 < count:
            v[2 * i + 1, ROWS:VR, :] = jnp.where(low, pltpu.roll(south, 4, 0), north)
    corner = jnp.where(iota((8, 128), 0) < HALO, cor_in[1], cor_in[0])
    edge = jnp.concatenate([col_in[...], corner], axis=0)
    lane = iota((VR, 128), 1)
    for f in range(count):
        own = v[f, :, 640:768]
        own = jnp.where((lane >= 80) & (lane < 84), pltpu.roll(edge, 80 - 8 * f, 1), own)
        own = jnp.where(lane >= 124, pltpu.roll(edge, 120 - 8 * f, 1), own)
        v[f, :, 640:768] = own


def kernel(
    flux_hbm,
    wet_hbm,
    w_hbm,
    owner_hbm,
    block_hbm,
    land_hbm,
    east_hbm,
    north_hbm,
    out_hbm,
    flux,
    wet,
    w,
    owner,
    block,
    land,
    east,
    north,
    items,
    index_v,
    index_s,
    labels,
    stage_a,
    stage_b,
    recv_a,
    recv_b,
    picked,
    grid_a,
    grid_b,
    coef,
    result,
    row_out,
    row_in,
    col_out,
    col_in,
    cor_in,
    in_sem,
    w_sem,
    f_sem,
    idx_sem,
    send_sem,
    recv_sem,
    halo_send,
    halo_recv,
    out_sem,
):
    tile, sub = lax.axis_index("tile"), lax.axis_index("sub")
    me = tile * 2 + sub

    small = []
    for i, (src, dst) in enumerate(
        (
            (owner_hbm, owner),
            (block_hbm, block),
            (wet_hbm, wet),
            (land_hbm, land),
            (east_hbm, east),
            (north_hbm, north),
        )
    ):
        copy = pltpu.make_async_copy(src, dst, in_sem.at[i])
        copy.start()
        small.append(copy)
    cells = OB * BLK // F_CHUNKS
    blocks = OB // W_CHUNKS
    flux_copies = [
        pltpu.make_async_copy(
            flux_hbm.at[:, :, pl.ds(i * cells, cells)],
            flux.at[:, :, pl.ds(i * cells, cells)],
            f_sem.at[i],
        )
        for i in range(F_CHUNKS)
    ]
    w_copies = [
        pltpu.make_async_copy(
            w_hbm.at[pl.ds(i * blocks, blocks)], w.at[pl.ds(i * blocks, blocks)], w_sem.at[i]
        )
        for i in range(W_CHUNKS)
    ]
    for i in range(W_CHUNKS):
        if i % (W_CHUNKS // F_CHUNKS) == 0:
            flux_copies[i // (W_CHUNKS // F_CHUNKS)].start()
        w_copies[i].start()

    barrier = pltpu.get_barrier_semaphore()

    def greet(i, carry):
        d = (me + i) % DEV
        pl.semaphore_signal(barrier, 1, device_id=(d // 2, d % 2), device_id_type=MESH)
        return carry

    lax.fori_loop(1, DEV, greet, 0)

    small[0].wait()
    small[1].wait()
    own = owner[...]
    blk = block[...]
    drow = iota((DEV, OB), 0)
    earlier = (iota((OB, OB), 0) < iota((OB, OB), 1)).astype(BF16)
    hit = [own[k : k + 1, :] == drow for k in range(2)]
    ones = [h.astype(F32) for h in hit]
    rank = [jnp.dot(o.astype(BF16), earlier, preferred_element_type=F32) for o in ones]
    rank[1] = rank[1] + jnp.sum(ones[0], axis=1, keepdims=True)
    wide = blk + (WIDE - ACROSS) * (
        (blk >= ACROSS).astype(jnp.int32)
        + (blk >= 2 * ACROSS).astype(jnp.int32)
        + (blk >= 3 * ACROSS).astype(jnp.int32)
    )
    wide = (wide + 1).astype(F32)
    position = iota((1, OB), 1).astype(F32) * 2.0
    first = iota((8, OB), 0)
    facts = []
    for k in range(2):
        facts.append(
            jnp.where(
                first == 0,
                wide[k : k + 1, :],
                jnp.where(first == 1, position + float(k - 2 * OB), 0.0),
            ).astype(BF16)
        )
    found = []
    for r in range(CAP):
        total = jnp.zeros((8, DEV), F32)
        for k in range(2):
            mine = jnp.where(rank[k] == float(r), ones[k], 0.0).astype(BF16)
            total = total + lax.dot_general(
                facts[k], mine, (((1,), (1,)), ((), ())), preferred_element_type=F32
            )
        found.append(total)
    row8 = iota((8, DEV), 0)
    index = jnp.zeros((8, DEV), F32)
    names = jnp.zeros((8, DEV), F32)
    for r in range(CAP):
        index = jnp.where(row8 == r, found[r][1:2, :] + float(2 * OB), index)
        names = jnp.where(row8 == r, found[r][0:1, :] - 1.0, names)
    index_v[...] = jnp.clip(index.astype(jnp.int32), 0, 2 * OB)
    to_smem = pltpu.make_async_copy(index_v, index_s, idx_sem)
    to_smem.start()
    labels[...] = jnp.concatenate([names, jnp.zeros((DEV - 8, DEV), F32)], axis=0).T

    coef[...] = jnp.zeros((2, VR, VC), F32)
    small[4].wait()
    small[5].wait()
    coef[0, 0:ROWS, 0:COLS] = east[...]
    row_global = tile * ROWS + iota((ROWS, COLS), 0)
    coef[1, 0:ROWS, 0:COLS] = jnp.where(row_global < 64 * ROWS - 1, north[...], 0.0)

    items[0, 2 * OB] = jnp.zeros((8, BLK), F32)
    items[1, 2 * OB] = jnp.zeros((8, BLK), F32)
    small[2].wait()
    frac = [np.float32(h) / np.float32(HOURS) for h in range(HOURS)]
    blank = jnp.zeros((1, BLK), F32)

    def contribute(p):
        at = pl.ds(pl.multiple_of(p * BLK, BLK), BLK)
        early = late = None
        for h in range(HOURS):
            x = flux[h, :, at].astype(F32)
            early = x if h == 0 else early + (np.float32(1.0) - frac[h]) * x
            if h:
                late = frac[h] * x if h == 1 else late + frac[h] * x
        mask = wet[pl.ds(p, 1), :].astype(F32)
        left = jnp.concatenate([early * mask, blank, late * mask, blank], axis=0).astype(BF16)
        for k in range(2):
            made = jnp.dot(left, w[p, k], preferred_element_type=F32)
            items[0, 2 * p + k] = made[0:8, :]
            items[1, 2 * p + k] = made[8:16, :]

    group = 8
    for i in range(W_CHUNKS):
        if i % (W_CHUNKS // F_CHUNKS) == 0:
            flux_copies[i // (W_CHUNKS // F_CHUNKS)].wait()
        w_copies[i].wait()

        def chunk(q, carry, i=i):
            for g in range(group):
                contribute(i * blocks + q * group + g)
            return carry

        lax.fori_loop(0, blocks // group, chunk, 0)

    to_smem.wait()
    pl.semaphore_wait(barrier, DEV - 1)

    coef_copies = halo_start(
        coef,
        2,
        tile,
        sub,
        row_out.at[0],
        row_in.at[0],
        col_out.at[0],
        col_in.at[0],
        cor_in.at[0],
        halo_send.at[0],
        halo_recv.at[0],
    )

    def pack(half, d, write):
        for r in range(CAP):
            write(r * FIELDS, items[half, index_s[r, d]][0:FIELDS, :])
        if half == 0:
            write(CAP * FIELDS, labels[pl.ds(d, 1), :])

    for half, stage, recv in ((0, stage_a, recv_a), (1, stage_b, recv_b)):

        def send(j, carry, half=half, stage=stage, recv=recv):
            t, u = peer_of(tile, sub, j)

            def write(row, value):
                stage[j, row : row + value.shape[0], :] = value

            pack(half, t * 2 + u, write)
            pltpu.make_async_remote_copy(
                src_ref=stage.at[j],
                dst_ref=recv.at[me],
                send_sem=send_sem.at[half],
                recv_sem=recv_sem.at[half],
                device_id=(t, u),
                device_id_type=MESH,
            ).start()
            return carry

        lax.fori_loop(1, DEV, send, 0)

    for half, recv in ((0, recv_a), (1, recv_b)):

        def write(row, value, recv=recv):
            recv[me, row : row + value.shape[0], :] = value

        pack(half, me, write)

    small[3].wait()
    halo_finish(coef_copies, coef, 2, row_in.at[0], col_in.at[0], cor_in.at[0])

    out_copies = []
    for half, stage, recv, grid in (
        (0, stage_a, recv_a, grid_a),
        (1, stage_b, recv_b, grid_b),
    ):
        everything = recv.at[pl.ds(0, DEV - 1)]
        pltpu.make_async_copy(everything, everything, recv_sem.at[half]).wait()
        if half == 0:
            named = recv[:, CAP * FIELDS, :].T
            rows = iota((4 * WIDE, DEV), 0).astype(F32)
            for r in range(CAP):
                picked[:, r * DEV : (r + 1) * DEV] = (rows == named[r : r + 1, :]).astype(BF16)
        for f in range(FIELDS):
            got = jnp.concatenate(
                [recv[:, r * FIELDS + f, :].astype(BF16) for r in range(CAP)], axis=0
            )
            sums = jnp.dot(picked[...], got, preferred_element_type=F32)
            tiles = swap_lanes_rows(sums.reshape(24, 8, 128))
            for r in range(4):
                for q in range(6):
                    at = slice(128 * q, 128 * q + 128)
                    value = tiles[6 * r + q]
                    if q < 5:
                        value = value * land[8 * r : 8 * r + 8, at].astype(F32)
                        grid[f, 8 * r : 8 * r + 8, at] = value
                    else:
                        sea = land[8 * r : 8 * r + 8, 640:720].astype(F32)
                        grid[f, 8 * r : 8 * r + 8, at] = value
                        grid[f, 8 * r : 8 * r + 8, 640:720] = value[:, 0:80] * sea
        copies = halo_start(
            grid,
            FIELDS,
            tile,
            sub,
            row_out.at[1 + half],
            row_in.at[1 + half],
            col_out.at[1 + half],
            col_in.at[1 + half],
            cor_in.at[1 + half],
            halo_send.at[1 + half],
            halo_recv.at[1 + half],
        )
        halo_finish(
            copies, grid, FIELDS, row_in.at[1 + half], col_in.at[1 + half], cor_in.at[1 + half]
        )

        def smooth(f, carry, grid=grid, half=half):
            v = grid[f]
            for turn in range(PASSES):
                flow = coef[0] * (pltpu.roll(v, VC - 1, 1) - v)
                rise = coef[1] * (pltpu.roll(v, VR - 1, 0) - v)
                v = v + (flow - pltpu.roll(flow, 1, 1)) + (rise - pltpu.roll(rise, 1, 0))
            result[half * FIELDS + f] = v[0:ROWS, 0:COLS]
            return carry

        lax.fori_loop(0, FIELDS, smooth, 0)
        span = pl.ds(half * FIELDS, FIELDS)
        copy = pltpu.make_async_copy(result.at[span], out_hbm.at[span], out_sem.at[half])
        copy.start()
        out_copies.append(copy)

    for half, stage in ((0, stage_a), (1, stage_b)):
        everything = stage.at[pl.ds(1, DEV - 1)]
        pltpu.make_async_copy(everything, everything, send_sem.at[half]).wait()
    for copy in out_copies:
        copy.wait()


def on_device(
    adjoint_flux,
    ocean_wet,
    intersection_weight,
    pair_owner,
    pair_block,
    land_sea,
    east_coef,
    north_coef,
):
    vmem = pltpu.VMEM
    dma = pltpu.SemaphoreType.DMA
    return pl.pallas_call(
        kernel,
        out_shape=jax.ShapeDtypeStruct((2 * FIELDS, ROWS, COLS), F32),
        in_specs=[pl.BlockSpec(memory_space=pl.ANY)] * 8,
        out_specs=pl.BlockSpec(memory_space=pl.ANY),
        scratch_shapes=[
            vmem((HOURS, FIELDS, OB * BLK), BF16),
            vmem((OB, BLK), jnp.int32),
            vmem((OB, 2, BLK, BLK), BF16),
            vmem((2, OB), jnp.int32),
            vmem((2, OB), jnp.int32),
            vmem((ROWS, COLS), jnp.int32),
            vmem((ROWS, COLS), F32),
            vmem((ROWS, COLS), F32),
            vmem((2, 2 * OB + 1, 8, BLK), F32),
            vmem((8, DEV), jnp.int32),
            pltpu.SMEM((8, DEV), jnp.int32),
            vmem((DEV, DEV), F32),
            vmem((DEV, CAP * FIELDS + 1, BLK), F32),
            vmem((DEV, CAP * FIELDS, BLK), F32),
            vmem((DEV, CAP * FIELDS + 1, BLK), F32),
            vmem((DEV, CAP * FIELDS, BLK), F32),
            vmem((4 * WIDE, CAP * DEV), BF16),
            vmem((FIELDS, VR, VC), F32),
            vmem((FIELDS, VR, VC), F32),
            vmem((2, VR, VC), F32),
            vmem((2 * FIELDS, ROWS, COLS), F32),
            vmem((3, 2, 4, 8, VC), F32),
            vmem((3, 2, 4, 8, VC), F32),
            vmem((3, ROWS, 128), F32),
            vmem((3, ROWS, 128), F32),
            vmem((3, 2, 8, 128), F32),
            dma((6,)),
            dma((W_CHUNKS,)),
            dma((F_CHUNKS,)),
            dma,
            dma((2,)),
            dma((2,)),
            dma((3, 5)),
            dma((3, 5)),
            dma((2,)),
        ],
        compiler_params=pltpu.CompilerParams(
            collective_id=0, has_side_effects=True, vmem_limit_bytes=60 * 2**20
        ),
        cost_estimate=pl.CostEstimate(
            flops=4 * 10**8, bytes_accessed=12 * 10**6, transcendentals=0
        ),
    )(
        adjoint_flux,
        ocean_wet.reshape(OB, BLK),
        intersection_weight,
        pair_owner.T,
        pair_block.T,
        land_sea,
        east_coef,
        north_coef,
    )


def solution(mesh):
    in_specs = (
        P(None, None, ("tile", "sub")),
        P(("tile", "sub")),
        P(("tile", "sub"), None, None, None),
        P(("tile", "sub"), None),
        P(("tile", "sub"), None),
        P("tile", "sub"),
        P("tile", "sub"),
        P("tile", "sub"),
    )
    out_specs = P(None, "tile", "sub")
    return jax.shard_map(
        on_device, mesh=mesh, in_specs=in_specs, out_specs=out_specs, check_vma=False
    )
```

time: 262 us -> 80.6 us (0.31)
  the two profiles are of different devices: /device:TPU:4 before, /device:TPU:1 now
where the time goes in v1:
time: 80.6 us; the launch traced here: 79.9 us
  Pallas kernels  77.4 us (96%)
  local copies, waits for them, and re-layouts  2.53 us (3%)
    pallas_call x1, Pallas kernels, on_device(): pl.pallas_call(kernel, out_shape=jax.ShapeDtypeStruct((2 * FIELDS, ROWS,...  77.4 us
    unnamed x1, local copies, waits for them, and re-layouts  2.53 us

profile of v1, /device:TPU:1, one launch (start us, length us, event | category | flops | bytes accessed | tf_op | source)
XLA Modules:
  0.0 79.9 jit_solution(15156927348271779885)
XLA Ops:
  0.0 77.4 %shard_map.82 = f32[14,32,720]{2,1,0:T(8,128)} custom-call(bf16[6,7,16384]{2,1,0:T(8,128)(2,1)} %flux_hbm.1, s32[128,128]{1,0:T(8,128)} %bitcast.3, bf16[128,2,128,128]{3,2,1,0:T(8,128)(2,1)} %w_hbm.1, s32[2,128]{1,0:T(2,128)} %bitcast.4, s32[2,128]{1,0:T(2,128)} %bitcast.5, s32[32,720]{1,0:T(8,128)} %land_hbm.1, f32[32,720]{1,0:T(8,128)} %east_hbm.1, ...), custom_call_target="tpu_custom_call" | custom-call | flops 400000000 | bytes 12000000 | tf_op jit(solution)/shard_map/pallas_call | solution.py:433
  77.4 2.5 %copy.10 = f32[14,32,720]{2,1,0:T(8,128)} copy(f32[14,32,720]{2,1,0:T(8,128)} %shard_map.82) | data formatting | bytes 2580480

commit v2 on v1

--- a/solution.py
+++ b/solution.py
@@ -13,6 +13,7 @@
 CAP = 4
 HOURS = 6
 FIELDS = 7
+PARTS = ((0, 8), (8, 6))
 BLK = 128
 OB = 128
 ROWS = 32
@@ -43,43 +44,52 @@
     return ((x * 4 + y) * 2 + z % 2) * 2 + c, z // 2
 
 
-def swap_lanes_rows(x):
-    s = iota(x.shape, 1)
-    g = iota(x.shape, 2) // 16
-    for m in (4, 2, 1):
-        sb = (s // m) % 2
-        gb = (g // m) % 2
-        up = pltpu.roll(pltpu.roll(x, 16 * m, 2), 8 - m, 1)
-        down = up if m == 4 else pltpu.roll(pltpu.roll(x, 128 - 16 * m, 2), m, 1)
-        x = jnp.where(sb < gb, up, jnp.where(sb > gb, down, x))
-    return x
-
-
-def halo_start(v, count, tile, sub, row_out, row_in, col_out, col_in, cor_in, send, recv):
-    low = iota((8, VC), 0) < HALO
-    for i in range((count + 1) // 2):
-        a, b = 2 * i, min(2 * i + 1, count - 1)
-        row_out[0, i] = jnp.where(low, pltpu.roll(v[a, 24:32, :], 4, 0), v[b, 24:32, :])
-        row_out[1, i] = jnp.where(low, v[a, 0:8, :], pltpu.roll(v[b, 0:8, :], 4, 0))
-    lane = iota((ROWS, 128), 1)
-    edge = jnp.zeros((ROWS, 128), F32)
-    for f in range(count):
-        left = v[f, 0:ROWS, 0:128]
-        right = v[f, 0:ROWS, 640:768]
-        if f:
-            left = pltpu.roll(left, 8 * f, 1)
-        right = pltpu.roll(right, (8 * f + 4 - 76) % 128, 1)
-        edge = jnp.where((lane >= 8 * f) & (lane < 8 * f + 4), left, edge)
-        edge = jnp.where((lane >= 8 * f + 4) & (lane < 8 * f + 8), right, edge)
-    col_out[...] = edge
+def swap_vregs_rows(xs):
+    s = iota((8, 128), 0)
+    xs = list(xs)
+    for m in (1, 2, 4):
+        low = (s // m) % 2 == 0
+        for a in range(8):
+            if (a // m) % 2 == 0:
+                p, q = xs[a], xs[a + m]
+                xs[a] = jnp.where(low, p, pltpu.roll(q, m, 0))
+                xs[a + m] = jnp.where(low, pltpu.roll(p, 8 - m, 0), q)
+    return xs
+
+
+def swap_vregs_lanes(xs):
+    g = iota((8, 128), 1) // 16
+    xs = list(xs)
+    for m in (1, 2, 4):
+        low = (g // m) % 2 == 0
+        for a in range(8):
+            if (a // m) % 2 == 0:
+                p, q = xs[a], xs[a + m]
+                xs[a] = jnp.where(low, p, pltpu.roll(q, 16 * m, 1))
+                xs[a + m] = jnp.where(low, pltpu.roll(p, 128 - 16 * m, 1), q)
+    return xs
+
+
+def halo_start(v, tile, sub, col_out, col_in, cor_in, send, recv):
+    lane = iota((8, 128), 1)
+    for n in range(2):
+        edge = jnp.zeros((8, 128), F32)
+        for i in range(16):
+            row = HALO + 16 * n + i
+            left, right = v[row, :, 0:128], v[row, :, 640:768]
+            if i:
+                left = pltpu.roll(left, 8 * i, 1)
+            right = pltpu.roll(right, (8 * i + 4 - 76) % 128, 1)
+            edge = jnp.where((lane >= 8 * i) & (lane < 8 * i + 4), left, edge)
+            edge = jnp.where((lane >= 8 * i + 4) & (lane < 8 * i + 8), right, edge)
+        col_out[n] = edge
     up, down, other = (tile + 1) % 64, (tile + 63) % 64, 1 - sub
-    n = (count + 1) // 2
     parts = (
-        (row_out.at[0, pl.ds(0, n)], row_in.at[0, pl.ds(0, n)], (up, sub)),
-        (row_out.at[1, pl.ds(0, n)], row_in.at[1, pl.ds(0, n)], (down, sub)),
+        (v.at[pl.ds(ROWS, HALO)], v.at[pl.ds(0, HALO)], (up, sub)),
+        (v.at[pl.ds(HALO, HALO)], v.at[pl.ds(HALO + ROWS, HALO)], (down, sub)),
         (col_out, col_in, (tile, other)),
-        (col_out.at[pl.ds(24, 8)], cor_in.at[0], (up, other)),
-        (col_out.at[pl.ds(0, 8)], cor_in.at[1], (down, other)),
+        (col_out.at[1], cor_in.at[0], (up, other)),
+        (col_out.at[0], cor_in.at[1], (down, other)),
     )
     copies = []
     for i, (src, dst, to) in enumerate(parts):
@@ -96,23 +106,23 @@
     return copies
 
 
-def halo_finish(copies, v, count, row_in, col_in, cor_in):
+def halo_finish(copies, v, col_in, cor_in):
     for copy in copies:
         copy.wait()
-    low = iota((8, VC), 0) < HALO
-    for i in range((count + 1) // 2):
-        south, north = row_in[1, i], row_in[0, i]
-        v[2 * i, ROWS:VR, :] = jnp.where(low, south, pltpu.roll(north, 4, 0))
-        if 2 * i + 1 < count:
-            v[2 * i + 1, ROWS:VR, :] = jnp.where(low, pltpu.roll(south, 4, 0), north)
-    corner = jnp.where(iota((8, 128), 0) < HALO, cor_in[1], cor_in[0])
-    edge = jnp.concatenate([col_in[...], corner], axis=0)
-    lane = iota((VR, 128), 1)
-    for f in range(count):
-        own = v[f, :, 640:768]
-        own = jnp.where((lane >= 80) & (lane < 84), pltpu.roll(edge, 80 - 8 * f, 1), own)
-        own = jnp.where(lane >= 124, pltpu.roll(edge, 120 - 8 * f, 1), own)
-        v[f, :, 640:768] = own
+    lane = iota((8, 128), 1)
+    for row in range(VR):
+        i = row - HALO
+        if i < 0:
+            edge, off = cor_in[0], 8 * ((ROWS + i) % 16)
+        elif i >= ROWS:
+            edge, off = cor_in[1], 8 * (i - ROWS)
+        else:
+            edge, off = col_in[i // 16], 8 * (i % 16)
+        own = v[row, :, 640:768]
+        after = pltpu.roll(edge, (80 - off) % 128, 1)
+        before = pltpu.roll(edge, (120 - off) % 128, 1)
+        own = jnp.where((lane >= 80) & (lane < 84), after, jnp.where(lane >= 124, before, own))
+        v[row, :, 640:768] = own
 
 
 def kernel(
@@ -142,12 +152,14 @@
     recv_a,
     recv_b,
     picked,
+    sums,
+    padded,
     grid_a,
     grid_b,
     coef,
+    east_b,
+    north_b,
     result,
-    row_out,
-    row_in,
     col_out,
     col_in,
     cor_in,
@@ -255,12 +267,22 @@
     to_smem.start()
     labels[...] = jnp.concatenate([names, jnp.zeros((DEV - 8, DEV), F32)], axis=0).T
 
-    coef[...] = jnp.zeros((2, VR, VC), F32)
+    padded[:, :, 640:VC] = jnp.zeros((3, ROWS, 128), F32)
     small[4].wait()
     small[5].wait()
-    coef[0, 0:ROWS, 0:COLS] = east[...]
+    padded[0, :, 0:COLS] = east[...]
     row_global = tile * ROWS + iota((ROWS, COLS), 0)
-    coef[1, 0:ROWS, 0:COLS] = jnp.where(row_global < 64 * ROWS - 1, north[...], 0.0)
+    padded[1, :, 0:COLS] = jnp.where(row_global < 64 * ROWS - 1, north[...], 0.0)
+    top = iota((8, VC), 0) == 0
+
+    def lay(r, carry):
+        at = pl.ds(pl.multiple_of(r * 8, 8), 8)
+        ease, norse = padded[0, at, :], padded[1, at, :]
+        for i in range(8):
+            coef[HALO + 8 * r + i] = jnp.where(top, ease[i : i + 1, :], norse[i : i + 1, :])
+        return carry
+
+    lax.fori_loop(0, ROWS // 8, lay, 0)
 
     items[0, 2 * OB] = jnp.zeros((8, BLK), F32)
     items[1, 2 * OB] = jnp.zeros((8, BLK), F32)
@@ -277,7 +299,7 @@
             if h:
                 late = frac[h] * x if h == 1 else late + frac[h] * x
         mask = wet[pl.ds(p, 1), :].astype(F32)
-        left = jnp.concatenate([early * mask, blank, late * mask, blank], axis=0).astype(BF16)
+        left = jnp.concatenate([early * mask, late * mask, blank, blank], axis=0).astype(BF16)
         for k in range(2):
             made = jnp.dot(left, w[p, k], preferred_element_type=F32)
             items[0, 2 * p + k] = made[0:8, :]
@@ -300,24 +322,15 @@
     pl.semaphore_wait(barrier, DEV - 1)
 
     coef_copies = halo_start(
-        coef,
-        2,
-        tile,
-        sub,
-        row_out.at[0],
-        row_in.at[0],
-        col_out.at[0],
-        col_in.at[0],
-        cor_in.at[0],
-        halo_send.at[0],
-        halo_recv.at[0],
+        coef, tile, sub, col_out.at[0], col_in.at[0], cor_in.at[0], halo_send.at[0], halo_recv.at[0]
     )
 
     def pack(half, d, write):
+        count = PARTS[half][1]
         for r in range(CAP):
-            write(r * FIELDS, items[half, index_s[r, d]][0:FIELDS, :])
+            write(r * count, items[half, index_s[r, d]][0:count, :])
         if half == 0:
-            write(CAP * FIELDS, labels[pl.ds(d, 1), :])
+            write(CAP * count, labels[pl.ds(d, 1), :])
 
     for half, stage, recv in ((0, stage_a, recv_a), (1, stage_b, recv_b)):
 
@@ -348,74 +361,109 @@
         pack(half, me, write)
 
     small[3].wait()
-    halo_finish(coef_copies, coef, 2, row_in.at[0], col_in.at[0], cor_in.at[0])
-
-    out_copies = []
-    for half, stage, recv, grid in (
-        (0, stage_a, recv_a, grid_a),
-        (1, stage_b, recv_b, grid_b),
-    ):
+    padded[2, :, 0:COLS] = land[...].astype(F32)
+    halo_finish(coef_copies, coef, col_in.at[0], cor_in.at[0])
+
+    def spread(i, carry):
+        both = coef[i]
+        east_b[i] = jnp.broadcast_to(both[0:1, :], (8, VC))
+        north_b[i] = jnp.broadcast_to(both[1:2, :], (8, VC))
+        return carry
+
+    lax.fori_loop(0, VR, spread, 0)
+
+    def assemble(half, recv, grid):
+        count = PARTS[half][1]
         everything = recv.at[pl.ds(0, DEV - 1)]
         pltpu.make_async_copy(everything, everything, recv_sem.at[half]).wait()
         if half == 0:
-            named = recv[:, CAP * FIELDS, :].T
+            named = recv[:, CAP * count, :].T
             rows = iota((4 * WIDE, DEV), 0).astype(F32)
             for r in range(CAP):
                 picked[:, r * DEV : (r + 1) * DEV] = (rows == named[r : r + 1, :]).astype(BF16)
-        for f in range(FIELDS):
+        for f in range(0, count, 2):
             got = jnp.concatenate(
-                [recv[:, r * FIELDS + f, :].astype(BF16) for r in range(CAP)], axis=0
+                [
+                    jnp.concatenate(
+                        [recv[:, r * count + f + e, :].astype(BF16) for r in range(CAP)], axis=0
+                    )
+                    for e in range(2)
+                ],
+                axis=1,
             )
-            sums = jnp.dot(picked[...], got, preferred_element_type=F32)
-            tiles = swap_lanes_rows(sums.reshape(24, 8, 128))
-            for r in range(4):
-                for q in range(6):
-                    at = slice(128 * q, 128 * q + 128)
-                    value = tiles[6 * r + q]
-                    if q < 5:
-                        value = value * land[8 * r : 8 * r + 8, at].astype(F32)
-                        grid[f, 8 * r : 8 * r + 8, at] = value
-                    else:
-                        sea = land[8 * r : 8 * r + 8, 640:720].astype(F32)
-                        grid[f, 8 * r : 8 * r + 8, at] = value
-                        grid[f, 8 * r : 8 * r + 8, 640:720] = value[:, 0:80] * sea
-        copies = halo_start(
+            both = jnp.dot(picked[...], got, preferred_element_type=F32)
+            sums[f] = both[:, 0:128]
+            sums[f + 1] = both[:, 128:256]
+        none = jnp.zeros((8, 128), F32)
+
+        def place(r, carry):
+            for q in range(6):
+                lanes = slice(128 * q, 128 * q + 128)
+                at = pl.ds(pl.multiple_of(r * WIDE + 8 * q, 8), 8)
+                xs = [sums[f, at, :] if f < count else none for f in range(8)]
+                xs = swap_vregs_lanes(swap_vregs_rows(xs))
+                sea = padded[2, pl.ds(pl.multiple_of(r * 8, 8), 8), lanes]
+                for i in range(8):
+                    grid[HALO + 8 * r + i, :, lanes] = xs[i] * sea[i : i + 1, :]
+            return carry
+
+        lax.fori_loop(0, ROWS // 8, place, 0)
+        return halo_start(
             grid,
-            FIELDS,
             tile,
             sub,
-            row_out.at[1 + half],
-            row_in.at[1 + half],
             col_out.at[1 + half],
             col_in.at[1 + half],
             cor_in.at[1 + half],
             halo_send.at[1 + half],
             halo_recv.at[1 + half],
         )
-        halo_finish(
-            copies, grid, FIELDS, row_in.at[1 + half], col_in.at[1 + half], cor_in.at[1 + half]
-        )
-
-        def smooth(f, carry, grid=grid, half=half):
-            v = grid[f]
-            for turn in range(PASSES):
-                flow = coef[0] * (pltpu.roll(v, VC - 1, 1) - v)
-                rise = coef[1] * (pltpu.roll(v, VR - 1, 0) - v)
-                v = v + (flow - pltpu.roll(flow, 1, 1)) + (rise - pltpu.roll(rise, 1, 0))
-            result[half * FIELDS + f] = v[0:ROWS, 0:COLS]
+
+    def smooth(half, copies, grid):
+        start, count = PARTS[half]
+        halo_finish(copies, grid, col_in.at[1 + half], cor_in.at[1 + half])
+        for turn in range(PASSES):
+            low, high = turn + 1, VR - 1 - turn
+            v = grid[low]
+            below = north_b[low - 1] * (v - grid[low - 1])
+
+            def line(i, carry):
+                v, below = carry
+                above = grid[i + 1]
+                rise = north_b[i] * (above - v)
+                flow = east_b[i] * (pltpu.roll(v, VC - 1, 1) - v)
+                grid[i] = v + (flow - pltpu.roll(flow, 1, 1)) + (rise - below)
+                return above, rise
+
+            lax.fori_loop(low, high, line, (v, below))
+
+        def turn_back(r, carry):
+            for q in range(6):
+                lanes = slice(128 * q, min(128 * q + 128, COLS))
+                xs = [grid[HALO + 8 * r + i, :, 128 * q : 128 * q + 128] for i in range(8)]
+                xs = swap_vregs_rows(xs)
+                for c in range(count):
+                    result[start + c, pl.ds(pl.multiple_of(r * 8, 8), 8), lanes] = xs[c][
+                        :, 0 : min(128, COLS - 128 * q)
+                    ]
             return carry
 
-        lax.fori_loop(0, FIELDS, smooth, 0)
-        span = pl.ds(half * FIELDS, FIELDS)
+        lax.fori_loop(0, ROWS // 8, turn_back, 0)
+        span = pl.ds(start, count)
         copy = pltpu.make_async_copy(result.at[span], out_hbm.at[span], out_sem.at[half])
         copy.start()
-        out_copies.append(copy)
+        return copy
+
+    halo_a = assemble(0, recv_a, grid_a)
+    halo_b = assemble(1, recv_b, grid_b)
+    out_a = smooth(0, halo_a, grid_a)
+    out_b = smooth(1, halo_b, grid_b)
 
     for half, stage in ((0, stage_a), (1, stage_b)):
         everything = stage.at[pl.ds(1, DEV - 1)]
         pltpu.make_async_copy(everything, everything, send_sem.at[half]).wait()
-    for copy in out_copies:
-        copy.wait()
+    out_a.wait()
+    out_b.wait()
 
 
 def on_device(
@@ -448,19 +496,21 @@
             vmem((8, DEV), jnp.int32),
             pltpu.SMEM((8, DEV), jnp.int32),
             vmem((DEV, DEV), F32),
-            vmem((DEV, CAP * FIELDS + 1, BLK), F32),
-            vmem((DEV, CAP * FIELDS, BLK), F32),
-            vmem((DEV, CAP * FIELDS + 1, BLK), F32),
-            vmem((DEV, CAP * FIELDS, BLK), F32),
+            vmem((DEV, CAP * PARTS[0][1] + 1, BLK), F32),
+            vmem((DEV, CAP * PARTS[1][1], BLK), F32),
+            vmem((DEV, CAP * PARTS[0][1] + 1, BLK), F32),
+            vmem((DEV, CAP * PARTS[1][1], BLK), F32),
             vmem((4 * WIDE, CAP * DEV), BF16),
-            vmem((FIELDS, VR, VC), F32),
-            vmem((FIELDS, VR, VC), F32),
-            vmem((2, VR, VC), F32),
+            vmem((8, 4 * WIDE, 128), F32),
+            vmem((3, ROWS, VC), F32),
+            vmem((VR, 8, VC), F32),
+            vmem((VR, 8, VC), F32),
+            vmem((VR, 8, VC), F32),
+            vmem((VR, 8, VC), F32),
+            vmem((VR, 8, VC), F32),
             vmem((2 * FIELDS, ROWS, COLS), F32),
-            vmem((3, 2, 4, 8, VC), F32),
-            vmem((3, 2, 4, 8, VC), F32),
-            vmem((3, ROWS, 128), F32),
-            vmem((3, ROWS, 128), F32),
+            vmem((3, 2, 8, 128), F32),
+            vmem((3, 2, 8, 128), F32),
             vmem((3, 2, 8, 128), F32),
             dma((6,)),
             dma((W_CHUNKS,)),

time: 80.6 us -> 112 us (1.39); the launches traced: 79.9 us -> 110 us
  Pallas kernels: 77.4 us -> 107 us
    pallas_call x1, Pallas kernels: 77.4 us -> 107 us  [on_device(): pl.pallas_call(kernel, out_shape=jax.ShapeDtypeStruct((2 * FIELDS, ROWS,...]
where the time goes in v2:
time: 112 us; the launch traced here: 110 us
  Pallas kernels  107 us (96%)
  local copies, waits for them, and re-layouts  2.53 us (2%)
    pallas_call x1, Pallas kernels, on_device(): pl.pallas_call(kernel, out_shape=jax.ShapeDtypeStruct((2 * FIELDS, ROWS,...  107 us
    unnamed x1, local copies, waits for them, and re-layouts  2.53 us

profile of v2, /device:TPU:1, one launch (start us, length us, event | category | flops | bytes accessed | tf_op | source)
XLA Modules:
  0.0 110.0 jit_solution(9550227415721589079)
XLA Ops:
  0.0 107.4 %shard_map.82 = f32[14,32,720]{2,1,0:T(8,128)} custom-call(bf16[6,7,16384]{2,1,0:T(8,128)(2,1)} %flux_hbm.1, s32[128,128]{1,0:T(8,128)} %bitcast.3, bf16[128,2,128,128]{3,2,1,0:T(8,128)(2,1)} %w_hbm.1, s32[2,128]{1,0:T(2,128)} %bitcast.4, s32[2,128]{1,0:T(2,128)} %bitcast.5, s32[32,720]{1,0:T(8,128)} %land_hbm.1, f32[32,720]{1,0:T(8,128)} %east_hbm.1, ...), custom_call_target="tpu_custom_call" | custom-call | flops 400000000 | bytes 12000000 | tf_op jit(solution)/shard_map/pallas_call | solution.py:481
  107.4 2.5 %copy.10 = f32[14,32,720]{2,1,0:T(8,128)} copy(f32[14,32,720]{2,1,0:T(8,128)} %shard_map.82) | data formatting | bytes 2580480

commit v3 on v2

--- a/solution.py
+++ b/solution.py
@@ -11,8 +11,11 @@
 PASSES = 4
 HALO = 4
 CAP = 4
+GROUPS = 4
+EACH = 32
 HOURS = 6
 FIELDS = 7
+CH = 14
 PARTS = ((0, 8), (8, 6))
 BLK = 128
 OB = 128
@@ -25,7 +28,7 @@
 DEV = 128
 STRIDE = 37
 W_CHUNKS = 8
-F_CHUNKS = 4
+F_CHUNKS = 8
 MESH = pl.DeviceIdType.MESH
 F32 = jnp.float32
 BF16 = jnp.bfloat16
@@ -70,7 +73,7 @@
     return xs
 
 
-def halo_start(v, tile, sub, col_out, col_in, cor_in, send, recv):
+def gather_edges(v, col_out):
     lane = iota((8, 128), 1)
     for n in range(2):
         edge = jnp.zeros((8, 128), F32)
@@ -83,6 +86,9 @@
             edge = jnp.where((lane >= 8 * i) & (lane < 8 * i + 4), left, edge)
             edge = jnp.where((lane >= 8 * i + 4) & (lane < 8 * i + 8), right, edge)
         col_out[n] = edge
+
+
+def halo_start(v, ready, tile, sub, col_out, col_in, cor_in, send, recv):
     up, down, other = (tile + 1) % 64, (tile + 63) % 64, 1 - sub
     parts = (
         (v.at[pl.ds(ROWS, HALO)], v.at[pl.ds(0, HALO)], (up, sub)),
@@ -93,6 +99,8 @@
     )
     copies = []
     for i, (src, dst, to) in enumerate(parts):
+        if i == 2 and not ready:
+            gather_edges(v, col_out)
         copy = pltpu.make_async_remote_copy(
             src_ref=src,
             dst_ref=dst,
@@ -147,18 +155,17 @@
     index_v,
     index_s,
     labels,
-    stage_a,
-    stage_b,
-    recv_a,
-    recv_b,
-    picked,
+    stage,
+    recv,
     sums,
     padded,
     grid_a,
     grid_b,
     coef,
     east_b,
+    west_b,
     north_b,
+    spare,
     result,
     col_out,
     col_in,
@@ -190,26 +197,20 @@
         copy = pltpu.make_async_copy(src, dst, in_sem.at[i])
         copy.start()
         small.append(copy)
-    cells = OB * BLK // F_CHUNKS
     blocks = OB // W_CHUNKS
-    flux_copies = [
-        pltpu.make_async_copy(
-            flux_hbm.at[:, :, pl.ds(i * cells, cells)],
-            flux.at[:, :, pl.ds(i * cells, cells)],
-            f_sem.at[i],
+    cells = blocks * BLK
+
+    def bring(i):
+        at = pl.ds(pl.multiple_of(i * cells, cells), cells)
+        ocean = pl.ds(i * blocks, blocks)
+        return (
+            pltpu.make_async_copy(flux_hbm.at[:, :, at], flux.at[:, :, at], f_sem.at[i]),
+            pltpu.make_async_copy(w_hbm.at[ocean], w.at[ocean], w_sem.at[i]),
         )
-        for i in range(F_CHUNKS)
-    ]
-    w_copies = [
-        pltpu.make_async_copy(
-            w_hbm.at[pl.ds(i * blocks, blocks)], w.at[pl.ds(i * blocks, blocks)], w_sem.at[i]
-        )
-        for i in range(W_CHUNKS)
-    ]
+
     for i in range(W_CHUNKS):
-        if i % (W_CHUNKS // F_CHUNKS) == 0:
-            flux_copies[i // (W_CHUNKS // F_CHUNKS)].start()
-        w_copies[i].start()
+        for copy in bring(i):
+            copy.start()
 
     barrier = pltpu.get_barrier_semaphore()
 
@@ -284,13 +285,15 @@
 
     lax.fori_loop(0, ROWS // 8, lay, 0)
 
+    gather_edges(coef, col_out.at[0])
+
     items[0, 2 * OB] = jnp.zeros((8, BLK), F32)
     items[1, 2 * OB] = jnp.zeros((8, BLK), F32)
     small[2].wait()
     frac = [np.float32(h) / np.float32(HOURS) for h in range(HOURS)]
     blank = jnp.zeros((1, BLK), F32)
 
-    def contribute(p):
+    def timed(p):
         at = pl.ds(pl.multiple_of(p * BLK, BLK), BLK)
         early = late = None
         for h in range(HOURS):
@@ -299,108 +302,106 @@
             if h:
                 late = frac[h] * x if h == 1 else late + frac[h] * x
         mask = wet[pl.ds(p, 1), :].astype(F32)
-        left = jnp.concatenate([early * mask, late * mask, blank, blank], axis=0).astype(BF16)
-        for k in range(2):
-            made = jnp.dot(left, w[p, k], preferred_element_type=F32)
-            items[0, 2 * p + k] = made[0:8, :]
-            items[1, 2 * p + k] = made[8:16, :]
-
-    group = 8
-    for i in range(W_CHUNKS):
-        if i % (W_CHUNKS // F_CHUNKS) == 0:
-            flux_copies[i // (W_CHUNKS // F_CHUNKS)].wait()
-        w_copies[i].wait()
-
-        def chunk(q, carry, i=i):
-            for g in range(group):
-                contribute(i * blocks + q * group + g)
-            return carry
-
-        lax.fori_loop(0, blocks // group, chunk, 0)
+        return jnp.concatenate([early * mask, late * mask, blank, blank], axis=0).astype(BF16)
+
+    nothing = jnp.zeros((16, BLK), BF16)
+
+    def chunk(i, carry):
+        for copy in bring(i):
+            copy.wait()
+        for g in range(0, blocks, 2):
+            p = i * blocks + g
+            left = jnp.concatenate(
+                [
+                    jnp.concatenate([timed(p), nothing], axis=1),
+                    jnp.concatenate([nothing, timed(p + 1)], axis=1),
+                ],
+                axis=0,
+            )
+            right = jnp.concatenate(
+                [jnp.concatenate([w[p + e, 0], w[p + e, 1]], axis=1) for e in range(2)], axis=0
+            )
+            made = jnp.dot(left, right, preferred_element_type=F32)
+            for e in range(2):
+                for k in range(2):
+                    for half in range(2):
+                        items[half, 2 * (p + e) + k] = made[
+                            16 * e + 8 * half : 16 * e + 8 * half + 8, BLK * k : BLK * k + BLK
+                        ]
+        return carry
+
+    lax.fori_loop(0, W_CHUNKS, chunk, 0)
 
     to_smem.wait()
     pl.semaphore_wait(barrier, DEV - 1)
 
     coef_copies = halo_start(
-        coef, tile, sub, col_out.at[0], col_in.at[0], cor_in.at[0], halo_send.at[0], halo_recv.at[0]
+        coef, True, tile, sub, col_out.at[0], col_in.at[0], cor_in.at[0], halo_send.at[0], halo_recv.at[0]
     )
 
-    def pack(half, d, write):
-        count = PARTS[half][1]
+    def pack(d, into):
         for r in range(CAP):
-            write(r * count, items[half, index_s[r, d]][0:count, :])
-        if half == 0:
-            write(CAP * count, labels[pl.ds(d, 1), :])
-
-    for half, stage, recv in ((0, stage_a, recv_a), (1, stage_b, recv_b)):
-
-        def send(j, carry, half=half, stage=stage, recv=recv):
+            at = index_s[r, d]
+            for half, (start, count) in enumerate(PARTS):
+                row = r * CH + start
+                into[row : row + count, :] = items[half, at][0:count, :]
+        into[CAP * CH : CAP * CH + 1, :] = labels[pl.ds(d, 1), :]
+
+    for g in range(GROUPS):
+
+        def send(j, carry, g=g):
             t, u = peer_of(tile, sub, j)
-
-            def write(row, value):
-                stage[j, row : row + value.shape[0], :] = value
-
-            pack(half, t * 2 + u, write)
+            pack(t * 2 + u, stage.at[j])
             pltpu.make_async_remote_copy(
                 src_ref=stage.at[j],
-                dst_ref=recv.at[me],
-                send_sem=send_sem.at[half],
-                recv_sem=recv_sem.at[half],
+                dst_ref=recv.at[j],
+                send_sem=send_sem,
+                recv_sem=recv_sem.at[g],
                 device_id=(t, u),
                 device_id_type=MESH,
             ).start()
             return carry
 
-        lax.fori_loop(1, DEV, send, 0)
-
-    for half, recv in ((0, recv_a), (1, recv_b)):
-
-        def write(row, value, recv=recv):
-            recv[me, row : row + value.shape[0], :] = value
-
-        pack(half, me, write)
+        lax.fori_loop(max(1, EACH * g), EACH * (g + 1), send, 0)
+
+    pack(me, recv.at[0])
 
     small[3].wait()
     padded[2, :, 0:COLS] = land[...].astype(F32)
-    halo_finish(coef_copies, coef, col_in.at[0], cor_in.at[0])
-
-    def spread(i, carry):
-        both = coef[i]
-        east_b[i] = jnp.broadcast_to(both[0:1, :], (8, VC))
-        north_b[i] = jnp.broadcast_to(both[1:2, :], (8, VC))
-        return carry
-
-    lax.fori_loop(0, VR, spread, 0)
-
-    def assemble(half, recv, grid):
-        count = PARTS[half][1]
-        everything = recv.at[pl.ds(0, DEV - 1)]
-        pltpu.make_async_copy(everything, everything, recv_sem.at[half]).wait()
-        if half == 0:
-            named = recv[:, CAP * count, :].T
-            rows = iota((4 * WIDE, DEV), 0).astype(F32)
-            for r in range(CAP):
-                picked[:, r * DEV : (r + 1) * DEV] = (rows == named[r : r + 1, :]).astype(BF16)
-        for f in range(0, count, 2):
+    slot_rows = iota((4 * WIDE, CAP * EACH), 0).astype(F32)
+
+    def add_group(g):
+        low = max(1, EACH * g)
+        everything = recv.at[pl.ds(low, EACH * (g + 1) - low)]
+        pltpu.make_async_copy(everything, everything, recv_sem.at[g]).wait()
+        here = slice(EACH * g, EACH * (g + 1))
+        named = recv[here, CAP * CH, :].T
+        line = jnp.concatenate([named[r : r + 1, :] for r in range(CAP)], axis=1)
+        picked = (slot_rows == line).astype(BF16)
+        for f in range(0, CH, 2):
             got = jnp.concatenate(
                 [
                     jnp.concatenate(
-                        [recv[:, r * count + f + e, :].astype(BF16) for r in range(CAP)], axis=0
+                        [recv[here, r * CH + f + e, :].astype(BF16) for r in range(CAP)], axis=0
                     )
                     for e in range(2)
                 ],
                 axis=1,
             )
-            both = jnp.dot(picked[...], got, preferred_element_type=F32)
-            sums[f] = both[:, 0:128]
-            sums[f + 1] = both[:, 128:256]
+            both = jnp.dot(picked, got, preferred_element_type=F32)
+            for e in range(2):
+                part = both[:, 128 * e : 128 * e + 128]
+                sums[f + e] = part if g == 0 else sums[f + e] + part
+
+    def assemble(half, grid):
+        start, count = PARTS[half]
         none = jnp.zeros((8, 128), F32)
 
         def place(r, carry):
             for q in range(6):
                 lanes = slice(128 * q, 128 * q + 128)
                 at = pl.ds(pl.multiple_of(r * WIDE + 8 * q, 8), 8)
-                xs = [sums[f, at, :] if f < count else none for f in range(8)]
+                xs = [sums[start + f, at, :] if f < count else none for f in range(8)]
                 xs = swap_vregs_lanes(swap_vregs_rows(xs))
                 sea = padded[2, pl.ds(pl.multiple_of(r * 8, 8), 8), lanes]
                 for i in range(8):
@@ -410,6 +411,7 @@
         lax.fori_loop(0, ROWS // 8, place, 0)
         return halo_start(
             grid,
+            False,
             tile,
             sub,
             col_out.at[1 + half],
@@ -422,20 +424,29 @@
     def smooth(half, copies, grid):
         start, count = PARTS[half]
         halo_finish(copies, grid, col_in.at[1 + half], cor_in.at[1 + half])
+        def lines(src, dst, base, n):
+            v = src[base]
+            below = north_b[base - 1] * (v - src[base - 1])
+            for k in range(n):
+                at = base + k
+                above = src[at + 1]
+                rise = north_b[at] * (above - v)
+                east_side = east_b[at] * (pltpu.roll(v, VC - 1, 1) - v)
+                west_side = west_b[at] * (v - pltpu.roll(v, 1, 1))
+                dst[at] = v + (east_side - west_side) + (rise - below)
+                v, below = above, rise
+
         for turn in range(PASSES):
-            low, high = turn + 1, VR - 1 - turn
-            v = grid[low]
-            below = north_b[low - 1] * (v - grid[low - 1])
-
-            def line(i, carry):
-                v, below = carry
-                above = grid[i + 1]
-                rise = north_b[i] * (above - v)
-                flow = east_b[i] * (pltpu.roll(v, VC - 1, 1) - v)
-                grid[i] = v + (flow - pltpu.roll(flow, 1, 1)) + (rise - below)
-                return above, rise
-
-            lax.fori_loop(low, high, line, (v, below))
+            src, dst = (grid, spare) if turn % 2 == 0 else (spare, grid)
+            low, count_rows = turn + 1, VR - 2 - 2 * turn
+
+            def block_of(n, carry, src=src, dst=dst, low=low):
+                lines(src, dst, low + 8 * n, 8)
+                return carry
+
+            lax.fori_loop(0, count_rows // 8, block_of, 0)
+            if count_rows % 8:
+                lines(src, dst, low + count_rows // 8 * 8, count_rows % 8)
 
         def turn_back(r, carry):
             for q in range(6):
@@ -454,14 +465,29 @@
         copy.start()
         return copy
 
-    halo_a = assemble(0, recv_a, grid_a)
-    halo_b = assemble(1, recv_b, grid_b)
+    add_group(0)
+    add_group(1)
+    halo_finish(coef_copies, coef, col_in.at[0], cor_in.at[0])
+
+    def spread(i, carry):
+        both = coef[i]
+        ease = jnp.broadcast_to(both[0:1, :], (8, VC))
+        east_b[i] = ease
+        west_b[i] = pltpu.roll(ease, 1, 1)
+        north_b[i] = jnp.broadcast_to(both[1:2, :], (8, VC))
+        return carry
+
+    lax.fori_loop(0, VR, spread, 0)
+
+    add_group(2)
+    add_group(3)
+    halo_a = assemble(0, grid_a)
+    halo_b = assemble(1, grid_b)
     out_a = smooth(0, halo_a, grid_a)
     out_b = smooth(1, halo_b, grid_b)
 
-    for half, stage in ((0, stage_a), (1, stage_b)):
-        everything = stage.at[pl.ds(1, DEV - 1)]
-        pltpu.make_async_copy(everything, everything, send_sem.at[half]).wait()
+    everything = stage.at[pl.ds(1, DEV - 1)]
+    pltpu.make_async_copy(everything, everything, send_sem).wait()
     out_a.wait()
     out_b.wait()
 
@@ -496,13 +522,12 @@
             vmem((8, DEV), jnp.int32),
             pltpu.SMEM((8, DEV), jnp.int32),
             vmem((DEV, DEV), F32),
-            vmem((DEV, CAP * PARTS[0][1] + 1, BLK), F32),
-            vmem((DEV, CAP * PARTS[1][1], BLK), F32),
-            vmem((DEV, CAP * PARTS[0][1] + 1, BLK), F32),
-            vmem((DEV, CAP * PARTS[1][1], BLK), F32),
-            vmem((4 * WIDE, CAP * DEV), BF16),
-            vmem((8, 4 * WIDE, 128), F32),
+            vmem((DEV, CAP * CH + 1, BLK), F32),
+            vmem((DEV, CAP * CH + 1, BLK), F32),
+            vmem((CH, 4 * WIDE, 128), F32),
             vmem((3, ROWS, VC), F32),
+            vmem((VR, 8, VC), F32),
+            vmem((VR, 8, VC), F32),
             vmem((VR, 8, VC), F32),
             vmem((VR, 8, VC), F32),
             vmem((VR, 8, VC), F32),
@@ -516,8 +541,8 @@
             dma((W_CHUNKS,)),
             dma((F_CHUNKS,)),
             dma,
-            dma((2,)),
-            dma((2,)),
+            dma,
+            dma((GROUPS,)),
             dma((3, 5)),
             dma((3, 5)),
             dma((2,)),

time: 112 us -> 78.6 us (0.70); the launches traced: 110 us -> 78.4 us
  Pallas kernels: 107 us -> 75.9 us
    pallas_call x1, Pallas kernels: 107 us -> 75.9 us  [on_device(): pl.pallas_call(kernel, out_shape=jax.ShapeDtypeStruct((2 * FIELDS, ROWS,...]
where the time goes in v3:
time: 78.6 us; the launch traced here: 78.4 us
  Pallas kernels  75.9 us (97%)
  local copies, waits for them, and re-layouts  2.53 us (3%)
    pallas_call x1, Pallas kernels, on_device(): pl.pallas_call(kernel, out_shape=jax.ShapeDtypeStruct((2 * FIELDS, ROWS,...  75.9 us
    unnamed x1, local copies, waits for them, and re-layouts  2.53 us

profile of v3, /device:TPU:1, one launch (start us, length us, event | category | flops | bytes accessed | tf_op | source)
XLA Modules:
  0.0 78.4 jit_solution(9247624318662817149)
XLA Ops:
  0.0 75.9 %shard_map.82 = f32[14,32,720]{2,1,0:T(8,128)} custom-call(bf16[6,7,16384]{2,1,0:T(8,128)(2,1)} %flux_hbm.1, s32[128,128]{1,0:T(8,128)} %bitcast.3, bf16[128,2,128,128]{3,2,1,0:T(8,128)(2,1)} %w_hbm.1, s32[2,128]{1,0:T(2,128)} %bitcast.4, s32[2,128]{1,0:T(2,128)} %bitcast.5, s32[32,720]{1,0:T(8,128)} %land_hbm.1, f32[32,720]{1,0:T(8,128)} %east_hbm.1, ...), custom_call_target="tpu_custom_call" | custom-call | flops 400000000 | bytes 12000000 | tf_op jit(solution)/shard_map/pallas_call | solution.py:507
  75.9 2.5 %copy.10 = f32[14,32,720]{2,1,0:T(8,128)} copy(f32[14,32,720]{2,1,0:T(8,128)} %shard_map.82) | data formatting | bytes 2580480

commit v4 on v3

--- a/solution.py
+++ b/solution.py
@@ -142,7 +142,7 @@
     land_hbm,
     east_hbm,
     north_hbm,
-    out_hbm,
+    out,
     flux,
     wet,
     w,
@@ -166,7 +166,6 @@
     west_b,
     north_b,
     spare,
-    result,
     col_out,
     col_in,
     cor_in,
@@ -178,7 +177,6 @@
     recv_sem,
     halo_send,
     halo_recv,
-    out_sem,
 ):
     tile, sub = lax.axis_index("tile"), lax.axis_index("sub")
     me = tile * 2 + sub
@@ -454,16 +452,12 @@
                 xs = [grid[HALO + 8 * r + i, :, 128 * q : 128 * q + 128] for i in range(8)]
                 xs = swap_vregs_rows(xs)
                 for c in range(count):
-                    result[start + c, pl.ds(pl.multiple_of(r * 8, 8), 8), lanes] = xs[c][
+                    out[start + c, pl.ds(pl.multiple_of(r * 8, 8), 8), lanes] = xs[c][
                         :, 0 : min(128, COLS - 128 * q)
                     ]
             return carry
 
         lax.fori_loop(0, ROWS // 8, turn_back, 0)
-        span = pl.ds(start, count)
-        copy = pltpu.make_async_copy(result.at[span], out_hbm.at[span], out_sem.at[half])
-        copy.start()
-        return copy
 
     add_group(0)
     add_group(1)
@@ -483,13 +477,11 @@
     add_group(3)
     halo_a = assemble(0, grid_a)
     halo_b = assemble(1, grid_b)
-    out_a = smooth(0, halo_a, grid_a)
-    out_b = smooth(1, halo_b, grid_b)
+    smooth(0, halo_a, grid_a)
+    smooth(1, halo_b, grid_b)
 
     everything = stage.at[pl.ds(1, DEV - 1)]
     pltpu.make_async_copy(everything, everything, send_sem).wait()
-    out_a.wait()
-    out_b.wait()
 
 
 def on_device(
@@ -506,9 +498,9 @@
     dma = pltpu.SemaphoreType.DMA
     return pl.pallas_call(
         kernel,
-        out_shape=jax.ShapeDtypeStruct((2 * FIELDS, ROWS, COLS), F32),
+        out_shape=pltpu.VMEM((2 * FIELDS, ROWS, COLS), F32),
         in_specs=[pl.BlockSpec(memory_space=pl.ANY)] * 8,
-        out_specs=pl.BlockSpec(memory_space=pl.ANY),
+        out_specs=pl.BlockSpec(memory_space=pltpu.VMEM),
         scratch_shapes=[
             vmem((HOURS, FIELDS, OB * BLK), BF16),
             vmem((OB, BLK), jnp.int32),
@@ -533,7 +525,6 @@
             vmem((VR, 8, VC), F32),
             vmem((VR, 8, VC), F32),
             vmem((VR, 8, VC), F32),
-            vmem((2 * FIELDS, ROWS, COLS), F32),
             vmem((3, 2, 8, 128), F32),
             vmem((3, 2, 8, 128), F32),
             vmem((3, 2, 8, 128), F32),
@@ -545,10 +536,9 @@
             dma((GROUPS,)),
             dma((3, 5)),
             dma((3, 5)),
-            dma((2,)),
         ],
         compiler_params=pltpu.CompilerParams(
-            collective_id=0, has_side_effects=True, vmem_limit_bytes=60 * 2**20
+            collective_id=0, has_side_effects=True, vmem_limit_bytes=54 * 2**20
         ),
         cost_estimate=pl.CostEstimate(
             flops=4 * 10**8, bytes_accessed=12 * 10**6, transcendentals=0

time: 78.6 us -> 76.2 us (0.969)
  local copies, waits for them, and re-layouts: 2.53 us -> 1.08 us
  Pallas kernels: 75.9 us -> 75 us
    unnamed x1, local copies, waits for them, and re-layouts: 2.53 us -> 1.08 us
    pallas_call x1, Pallas kernels: 75.9 us -> 75 us  [on_device(): pl.pallas_call(kernel, out_shape=pltpu.VMEM((2 * FIELDS, ROWS, COLS), F32...]
where the time goes in v4:
time: 76.2 us; the launch traced here: 76.1 us
  Pallas kernels  75 us (98%)
  local copies, waits for them, and re-layouts  1.08 us (1%)
    pallas_call x1, Pallas kernels, on_device(): pl.pallas_call(kernel, out_shape=pltpu.VMEM((2 * FIELDS, ROWS, COLS), F32...  75 us

profile of v4, /device:TPU:1, one launch (start us, length us, event | category | flops | bytes accessed | tf_op | source)
XLA Modules:
  0.0 76.1 jit_solution(18222421252473592771)
XLA Ops:
  0.0 75.0 %shard_map.82 = f32[14,32,720]{2,1,0:T(8,128)S(1)} custom-call(bf16[6,7,16384]{2,1,0:T(8,128)(2,1)} %flux_hbm.1, s32[128,128]{1,0:T(8,128)} %bitcast.3, bf16[128,2,128,128]{3,2,1,0:T(8,128)(2,1)} %w_hbm.1, s32[2,128]{1,0:T(2,128)} %bitcast.4, s32[2,128]{1,0:T(2,128)} %bitcast.5, s32[32,720]{1,0:T(8,128)} %land_hbm.1, f32[32,720]{1,0:T(8,128)} %east_hbm.1, ...), custom_call_target="tpu_custom_call" | custom-call | flops 400000000 | bytes 12000000 | tf_op jit(solution)/shard_map/pallas_call | solution.py:499
  75.1 1.1 %copy.10 = f32[14,32,720]{2,1,0:T(8,128)} copy(f32[14,32,720]{2,1,0:T(8,128)S(1)} %shard_map.82) | data formatting | bytes 2580480

commit v5 on v4

--- a/solution.py
+++ b/solution.py
@@ -26,7 +26,7 @@
 VR = ROWS + 8
 VC = 768
 DEV = 128
-STRIDE = 37
+STRIDE = 53
 W_CHUNKS = 8
 F_CHUNKS = 8
 MESH = pl.DeviceIdType.MESH
@@ -368,15 +368,18 @@
     padded[2, :, 0:COLS] = land[...].astype(F32)
     slot_rows = iota((4 * WIDE, CAP * EACH), 0).astype(F32)
 
-    def add_group(g):
+    def arrive(g):
         low = max(1, EACH * g)
         everything = recv.at[pl.ds(low, EACH * (g + 1) - low)]
         pltpu.make_async_copy(everything, everything, recv_sem.at[g]).wait()
         here = slice(EACH * g, EACH * (g + 1))
         named = recv[here, CAP * CH, :].T
         line = jnp.concatenate([named[r : r + 1, :] for r in range(CAP)], axis=1)
-        picked = (slot_rows == line).astype(BF16)
-        for f in range(0, CH, 2):
+        return (slot_rows == line).astype(BF16)
+
+    def add_group(g, picked, first, last):
+        here = slice(EACH * g, EACH * (g + 1))
+        for f in range(first, last, 2):
             got = jnp.concatenate(
                 [
                     jnp.concatenate(
@@ -459,8 +462,16 @@
 
         lax.fori_loop(0, ROWS // 8, turn_back, 0)
 
-    add_group(0)
-    add_group(1)
+    for g in range(GROUPS // 2):
+        add_group(g, arrive(g), 0, CH)
+    for g in range(GROUPS // 2, GROUPS - 1):
+        add_group(g, arrive(g), 0, CH)
+    final = arrive(GROUPS - 1)
+    halves = []
+    for half, grid in ((0, grid_a), (1, grid_b)):
+        start, count = PARTS[half]
+        add_group(GROUPS - 1, final, start, start + count)
+        halves.append(assemble(half, grid))
     halo_finish(coef_copies, coef, col_in.at[0], cor_in.at[0])
 
     def spread(i, carry):
@@ -473,12 +484,8 @@
 
     lax.fori_loop(0, VR, spread, 0)
 
-    add_group(2)
-    add_group(3)
-    halo_a = assemble(0, grid_a)
-    halo_b = assemble(1, grid_b)
-    smooth(0, halo_a, grid_a)
-    smooth(1, halo_b, grid_b)
+    smooth(0, halves[0], grid_a)
+    smooth(1, halves[1], grid_b)
 
     everything = stage.at[pl.ds(1, DEV - 1)]
     pltpu.make_async_copy(everything, everything, send_sem).wait()

time: 76.2 us -> 73.9 us (0.970)
  Pallas kernels: 75 us -> 72.7 us
    pallas_call x1, Pallas kernels: 75 us -> 72.7 us  [on_device(): pl.pallas_call(kernel, out_shape=pltpu.VMEM((2 * FIELDS, ROWS, COLS), F32...]
where the time goes in v5:
time: 73.9 us; the launch traced here: 73.8 us
  Pallas kernels  72.7 us (98%)
  local copies, waits for them, and re-layouts  1.08 us (1%)
    pallas_call x1, Pallas kernels, on_device(): pl.pallas_call(kernel, out_shape=pltpu.VMEM((2 * FIELDS, ROWS, COLS), F32...  72.7 us

profile of v5, /device:TPU:1, one launch (start us, length us, event | category | flops | bytes accessed | tf_op | source)
XLA Modules:
  0.0 73.8 jit_solution(7934533541112193596)
XLA Ops:
  0.0 72.7 %shard_map.82 = f32[14,32,720]{2,1,0:T(8,128)S(1)} custom-call(bf16[6,7,16384]{2,1,0:T(8,128)(2,1)} %flux_hbm.1, s32[128,128]{1,0:T(8,128)} %bitcast.3, bf16[128,2,128,128]{3,2,1,0:T(8,128)(2,1)} %w_hbm.1, s32[2,128]{1,0:T(2,128)} %bitcast.4, s32[2,128]{1,0:T(2,128)} %bitcast.5, s32[32,720]{1,0:T(8,128)} %land_hbm.1, f32[32,720]{1,0:T(8,128)} %east_hbm.1, ...), custom_call_target="tpu_custom_call" | custom-call | flops 400000000 | bytes 12000000 | tf_op jit(solution)/shard_map/pallas_call | solution.py:506
  72.7 1.1 %copy.10 = f32[14,32,720]{2,1,0:T(8,128)} copy(f32[14,32,720]{2,1,0:T(8,128)S(1)} %shard_map.82) | data formatting | bytes 2580480

commit v6 on v5

--- a/solution.py
+++ b/solution.py
@@ -333,10 +333,6 @@
     to_smem.wait()
     pl.semaphore_wait(barrier, DEV - 1)
 
-    coef_copies = halo_start(
-        coef, True, tile, sub, col_out.at[0], col_in.at[0], cor_in.at[0], halo_send.at[0], halo_recv.at[0]
-    )
-
     def pack(d, into):
         for r in range(CAP):
             at = index_s[r, d]
@@ -362,6 +358,9 @@
 
         lax.fori_loop(max(1, EACH * g), EACH * (g + 1), send, 0)
 
+    coef_copies = halo_start(
+        coef, True, tile, sub, col_out.at[0], col_in.at[0], cor_in.at[0], halo_send.at[0], halo_recv.at[0]
+    )
     pack(me, recv.at[0])
 
     small[3].wait()

time: 73.9 us -> 73.5 us (level)
  no operation moved by 1% of the time
where the time goes in v6:
time: 73.5 us; the launch traced here: 73.4 us
  Pallas kernels  72.3 us (98%)
  local copies, waits for them, and re-layouts  1.08 us (1%)
    pallas_call x1, Pallas kernels, on_device(): pl.pallas_call(kernel, out_shape=pltpu.VMEM((2 * FIELDS, ROWS, COLS), F32...  72.3 us

profile of v6, /device:TPU:1, one launch (start us, length us, event | category | flops | bytes accessed | tf_op | source)
XLA Modules:
  0.0 73.4 jit_solution(16569083376073452263)
XLA Ops:
  0.0 72.3 %shard_map.82 = f32[14,32,720]{2,1,0:T(8,128)S(1)} custom-call(bf16[6,7,16384]{2,1,0:T(8,128)(2,1)} %flux_hbm.1, s32[128,128]{1,0:T(8,128)} %bitcast.3, bf16[128,2,128,128]{3,2,1,0:T(8,128)(2,1)} %w_hbm.1, s32[2,128]{1,0:T(2,128)} %bitcast.4, s32[2,128]{1,0:T(2,128)} %bitcast.5, s32[32,720]{1,0:T(8,128)} %land_hbm.1, f32[32,720]{1,0:T(8,128)} %east_hbm.1, ...), custom_call_target="tpu_custom_call" | custom-call | flops 400000000 | bytes 12000000 | tf_op jit(solution)/shard_map/pallas_call | solution.py:505
  72.3 1.1 %copy.10 = f32[14,32,720]{2,1,0:T(8,128)} copy(f32[14,32,720]{2,1,0:T(8,128)S(1)} %shard_map.82) | data formatting | bytes 2580480
